TPU v7x, 256 devices: a whole 4x4x8 slice. The times are simulated.
256 devices in a mesh: rows: 128 (over x, z, y), sub: 2 (over core).
Axes of the slice: x: 4, y: 4, z: 8, core: 2. Of those that a mesh axis runs over, the one named last changes fastest.
Arguments:
- upper_tiles: bfloat16 [8192, 64, 256], P('rows', None, 'sub'), may hold values from 0 to 1
- tile_clusters: int32 [8192, 4], P('rows', 'sub'), may hold values from 0 to 8191, as said below
- cluster_slot: int32 [8192], replicated, may hold values from 0 to 8191, as said below
- start_block: float32 [16, 524288], P('sub', 'rows'), may hold values from -6 to 6
Outputs:
- basis: float32 [2, 16, 524288], P(None, 'sub', 'rows')
- coefficients: float32 [4, 16, 16], replicated
Inputs may be any that keep to these rules, and one draw needn't show every extreme that they name: `cluster_slot`: a permutation of 0 to 8191. `tile_clusters`: for each index of rows and each tile pair (tiles 0 and 1, or 2 and 3) of its block rows, at most 3 tiles have their column block cluster_slot[id] on rows index cluster_slot[id] // 64; some such count equals 3.
All inputs are finite; a program needn't handle non-finite values.
Results may differ from a plain program's by a relative error of at most 0.0029.
Values may be sent and summed in bfloat16 or wider, within the bound.
A program may use at most 64 MiB of HBM per device.

v0:
```python
import math

import jax
import jax.numpy as jnp
from jax import lax
from jax.sharding import PartitionSpec as P

STEPS = 2


def inner(left, right):
    return jnp.dot(left, right.T, precision=lax.Precision.HIGHEST)


def times(left, right):
    return jnp.dot(left, right, precision=lax.Precision.HIGHEST)


def local(upper_tiles, tile_clusters, cluster_slot, start_block):
    blocks = upper_tiles.shape[0]
    cluster = upper_tiles.shape[1]
    groups = lax.axis_size("rows")
    capacity = 2 * blocks // groups + 2
    held_tiles, held_ids = (upper_tiles, tile_clusters)
    per_row = held_tiles.shape[2] // cluster
    stacked = held_tiles.reshape(blocks, cluster, per_row, cluster).transpose(0, 2, 1, 3)
    targets = cluster_slot[held_ids].reshape(-1)
    owners = targets // blocks
    local_block = targets % blocks
    count = owners.shape[0]
    order = jnp.arange(count, dtype=jnp.int32)
    before = (owners[:, None] == owners[None, :]) & (order[None, :] < order[:, None])
    ranks = jnp.sum(before.astype(jnp.int32), axis=1)
    slots = owners * capacity + ranks
    request = jnp.zeros((groups * capacity,), jnp.int32).at[slots].set(local_block)
    asked = lax.all_to_all(
        request.reshape(groups, capacity), "rows", split_axis=0, concat_axis=0, tiled=True
    ).reshape(-1)
    own_degree = jnp.sum(stacked, axis=(1, 3), dtype=jnp.float32)
    tile_columns = jnp.sum(stacked, axis=2, dtype=jnp.float32).reshape(count, cluster)
    column_out = jnp.zeros((groups * capacity, cluster), jnp.float32).at[slots].set(tile_columns)
    column_back = lax.all_to_all(
        column_out.reshape(groups, capacity, cluster),
        "rows",
        split_axis=0,
        concat_axis=0,
        tiled=True,
    )
    degree = own_degree.at[asked].add(column_back.reshape(groups * capacity, cluster))
    degree = lax.psum(degree, "sub")
    scale = lax.rsqrt(degree.reshape(blocks * cluster))
    full_start = lax.all_gather(start_block, "sub", axis=0, tiled=True)
    first = lax.psum(inner(full_start, full_start), "rows")
    lower = jnp.linalg.cholesky(first)
    current = lax.linalg.triangular_solve(lower, full_start, left_side=True, lower=True)
    previous = jnp.zeros_like(current)
    link = jnp.zeros_like(first)
    nodes = blocks * cluster * groups
    half_rows = start_block.shape[0]
    bases = []
    coeffs = []
    for step in range(STEPS):
        width_k = current.shape[0]
        scaled = (current * scale[None, :]).astype(jnp.bfloat16)
        scaled = scaled.reshape(width_k, blocks, cluster).transpose(1, 0, 2)
        reply = scaled[asked].reshape(groups, capacity, width_k * cluster)
        fetched = lax.all_to_all(reply, "rows", split_axis=0, concat_axis=0, tiled=True).reshape(
            groups * capacity, width_k, cluster
        )
        partner = fetched[slots].reshape(blocks, per_row, width_k, cluster)
        forward = jnp.einsum("bwkc,bwrc->bkr", partner, stacked, preferred_element_type=jnp.float32)
        mirrored = jnp.einsum("bkr,bwrc->bwkc", scaled, stacked, preferred_element_type=jnp.float32)
        mirrored = mirrored.reshape(count, width_k, cluster)
        outgoing = (
            jnp.zeros((groups * capacity, width_k, cluster), jnp.float32).at[slots].set(mirrored)
        )
        returned = lax.all_to_all(
            outgoing.reshape(groups, capacity, width_k * cluster),
            "rows",
            split_axis=0,
            concat_axis=0,
            tiled=True,
        )
        returned = returned.reshape(groups * capacity, width_k, cluster)
        summed = forward.at[asked].add(returned)
        product = summed.transpose(1, 0, 2).reshape(width_k, blocks * cluster)
        product = lax.psum(product, "sub")
        applied = current - scale[None, :] * product
        alpha = lax.psum(inner(current, applied), "rows")
        residual = applied - times(alpha.T, current) - times(link.T, previous)
        gram = lax.psum(inner(residual, residual), "rows")
        lower = jnp.linalg.cholesky(gram)
        following = lax.linalg.triangular_solve(lower, residual, left_side=True, lower=True)
        coeffs.append(alpha)
        coeffs.append(lower.T)
        own_rows = lax.dynamic_slice_in_dim(
            following, lax.axis_index("sub") * half_rows, half_rows, 0
        )
        bases.append(own_rows * math.sqrt(nodes))
        previous, current, link = (current, following, lower)
    return (jnp.stack(bases), jnp.stack(coeffs))


def solution(mesh):
    in_specs = (P("rows", None, "sub"), P("rows", "sub"), P(), P("sub", "rows"))
    out_specs = (P(None, "sub", "rows"), P())
    return jax.shard_map(local, mesh=mesh, in_specs=in_specs, out_specs=out_specs, check_vma=False)
```

profile of v0, /device:TPU:8, one launch (start us, length us, event | category | flops | bytes accessed | tf_op | source)
XLA Modules:
  0.0 2155.0 jit_solution(1661766208840879476)
XLA Ops:
  11.3 15.3 all-to-all-start
  28.4 2.0 all_gather.3
  30.8 348.1 %psum.56 = f32[16,16]{0,1:T(8,128)S(1)} all-reduce(f32[16,16]{0,1:T(8,128)S(1)} %fusion.57), channel_id=1, replica_groups=mesh['rows'=128,'sub'=2] {'rows'}, use_global_device_ids=true, to_apply=%region_0.1 | all-reduce | flops 256 | bytes 2048 | tf_op jit(solution)/shard_map/psum | solution.py:53
  379.0 1.5 cholesky.59
  384.9 11.6 all-to-all-start.1
  398.1 10.0 all-to-all-done.1
  409.8 2.7 scatter_fusion
  412.5 3.6 psum.57
  417.0 2.6 gather_fusion.1
  419.6 4.1 reshape.257
  423.7 7.8 all-to-all-start.2
  431.5 1.4 fusion.4
  432.9 1.9 broadcast.191.clone
  434.8 15.4 scatter_fusion.1
  450.2 4.5 reshape.261
  454.7 6.7 all-to-all-done.2
  461.3 8.3 all-to-all-start.3
  469.7 3.9 reshape.258
  473.6 2.1 gather_fusion.2
  476.4 44.5 %all-to-all-done.3 = f32[128,3,1024]{2,1,0:T(4,128)} async-done(((f32[128,3,1024]{2,1,0:T(4,128)}), f32[128,3,1024]{2,1,0:T(4,128)}, u32[]{:S(2)}, u32[]{:S(2)}) %all-to-all-start.3) | async-done | bytes 1572896 | tf_op jit(solution)/shard_map/all_to_all | solution.py:77
  520.9 4.5 reshape.352
  525.4 31.1 %scatter_fusion.2 = f32[64,16,64]{2,1,0:T(8,128)S(1)} fusion(f32[64,16,64]{2,1,0:T(8,128)S(1)} %fusion.8, s32[384]{0:T(512)S(1)} %fusion.50, f32[384,16,64]{2,1,0:T(8,128)} %reshape.352), kind=kCustom, calls=%fused_computation.9 | custom fusion | flops 393216 | bytes 4720128 | tf_op jit(solution)/shard_map/scatter-add | solution.py:85
  557.6 24.8 %all-reduce.3.cloned.1.call-done = f32[16,4096]{1,0:T(8,128)} async-done(((f32[16,4096]{1,0:T(8,128)}), f32[16,4096]{1,0:T(8,128)}) %all-reduce.3.cloned.1.call-update) | async-done | bytes 262160 | tf_op jit(solution)/shard_map/psum | solution.py:87
  582.4 1.4 fusion.21
  583.8 347.8 %psum.59 = f32[16,16]{0,1:T(8,128)S(1)} all-reduce(f32[16,16]{0,1:T(8,128)S(1)} %fusion.21), channel_id=1, replica_groups=mesh['rows'=128,'sub'=2] {'rows'}, use_global_device_ids=true, to_apply=%region_13.16 | all-reduce | flops 256 | bytes 2048 | tf_op jit(solution)/shard_map/psum | solution.py:89
  931.6 1.3 convolution_subtract_fusion.3
  933.7 356.4 %psum.60 = f32[16,16]{0,1:T(8,128)S(1)} all-reduce(f32[16,16]{0,1:T(8,128)S(1)} %fusion.58), channel_id=1, replica_groups=mesh['rows'=128,'sub'=2] {'rows'}, use_global_device_ids=true, to_apply=%region_14.17 | all-reduce | flops 256 | bytes 2048 | tf_op jit(solution)/shard_map/psum | solution.py:91
  1290.2 1.5 cholesky.70
  1295.0 2.6 gather_fusion.3
  1297.6 4.1 reshape.265
  1301.7 6.4 all-to-all-start.4
  1308.1 1.4 fusion
  1309.5 1.9 broadcast.191
  1311.4 15.4 scatter_fusion.3
  1326.8 4.5 reshape.269
  1331.3 14.2 all-to-all-start.5
  1345.6 3.9 reshape.266
  1349.6 2.9 gather_fusion.4
  1352.4 1.7 fusion.11
  1354.1 21.2 all-to-all-done.5
  1375.3 4.5 reshape.368
  1379.9 31.1 %scatter_fusion.4 = f32[64,16,64]{2,1,0:T(8,128)S(1)} fusion(f32[64,16,64]{2,1,0:T(8,128)S(1)} %fusion.11, s32[384]{0:T(512)S(1)} %fusion.50, f32[384,16,64]{2,1,0:T(8,128)} %reshape.368), kind=kCustom, calls=%fused_computation.11 | custom fusion | flops 393216 | bytes 4720128 | tf_op jit(solution)/shard_map/scatter-add | solution.py:85
  1412.1 25.2 %all-reduce.5.cloned.1.call-done = f32[16,4096]{1,0:T(8,128)} async-done(((f32[16,4096]{1,0:T(8,128)}), f32[16,4096]{1,0:T(8,128)}) %all-reduce.5.cloned.1.call-update) | async-done | bytes 262160 | tf_op jit(solution)/shard_map/psum | solution.py:87
  1437.3 1.4 fusion.20
  1438.7 347.9 %psum.62 = f32[16,16]{0,1:T(8,128)S(1)} all-reduce(f32[16,16]{0,1:T(8,128)S(1)} %fusion.20), channel_id=1, replica_groups=mesh['rows'=128,'sub'=2] {'rows'}, use_global_device_ids=true, to_apply=%region_18.21 | all-reduce | flops 256 | bytes 2048 | tf_op jit(solution)/shard_map/psum | solution.py:89
  1786.6 1.3 convolution_subtract_fusion.1
  1789.4 352.8 %psum.63 = f32[16,16]{0,1:T(8,128)S(1)} all-reduce(f32[16,16]{0,1:T(8,128)S(1)} %fusion.59), channel_id=1, replica_groups=mesh['rows'=128,'sub'=2] {'rows'}, use_global_device_ids=true, to_apply=%region_19.22 | all-reduce | flops 256 | bytes 2048 | tf_op jit(solution)/shard_map/psum | solution.py:91
  2142.3 1.5 cholesky.81
  (79 shorter events, 28.0 us)
Async XLA Ops:
  7.2 1.0 copy-start
  8.1 18.5 copy-start.1
  11.3 373.6 %all-to-all-start = ((s32[128,1,3]{2,1,0:T(1,128)}), s32[128,1,3]{2,1,0:T(1,128)S(1)}, u32[]{:S(2)}, u32[]{:S(2)}) async-start(s32[128,1,3]{2,1,0:T(1,128)} %bitcast.7), calls=%async_computation | async-start | bytes 131072 | tf_op jit(solution)/shard_map/all_to_all | solution.py:36
  26.7 1.7 copy-start.2
  384.9 23.2 %all-to-all-start.1 = ((f32[128,1,192]{2,1,0:T(1,128)}), f32[128,1,192]{2,1,0:T(1,128)S(1)}, u32[]{:S(2)}, u32[]{:S(2)}) async-start(f32[128,1,192]{2,1,0:T(1,128)} %reshape.400), calls=%async_computation.1 | async-start | bytes 262144 | tf_op jit(solution)/shard_map/all_to_all | solution.py:42
  423.7 37.7 %all-to-all-start.2 = ((bf16[128,3,1024]{2,1,0:T(4,128)(2,1)}), bf16[128,3,1024]{2,1,0:T(4,128)(2,1)}, u32[]{:S(2)}, u32[]{:S(2)}) async-start(bf16[128,3,1024]{2,1,0:T(4,128)(2,1)} %reshape.257), calls=%async_computation.2 | async-start | bytes 2097152 | tf_op jit(solution)/shard_map/all_to_all | solution.py:67
  461.3 59.5 %all-to-all-start.3 = ((f32[128,3,1024]{2,1,0:T(4,128)}), f32[128,3,1024]{2,1,0:T(4,128)}, u32[]{:S(2)}, u32[]{:S(2)}) async-start(f32[128,3,1024]{2,1,0:T(4,128)} %reshape.261), calls=%async_computation.3 | async-start | bytes 4194304 | tf_op jit(solution)/shard_map/all_to_all | solution.py:77
  469.6 112.8 %all-reduce.3.cloned.1.call-start = ((), (), s32[]{:S(2)}) async-start(), calls=%async_computation.6 | async-start | bytes 524288 | tf_op jit(solution)/shard_map/psum | solution.py:87
  1301.7 29.7 %all-to-all-start.4 = ((bf16[128,3,1024]{2,1,0:T(4,128)(2,1)}), bf16[128,3,1024]{2,1,0:T(4,128)(2,1)}, u32[]{:S(2)}, u32[]{:S(2)}) async-start(bf16[128,3,1024]{2,1,0:T(4,128)(2,1)} %reshape.265), calls=%async_computation.4 | async-start | bytes 2097152 | tf_op jit(solution)/shard_map/all_to_all | solution.py:67
  1331.3 44.0 %all-to-all-start.5 = ((f32[128,3,1024]{2,1,0:T(4,128)}), f32[128,3,1024]{2,1,0:T(4,128)}, u32[]{:S(2)}, u32[]{:S(2)}) async-start(f32[128,3,1024]{2,1,0:T(4,128)} %reshape.269), calls=%async_computation.5 | async-start | bytes 4194304 | tf_op jit(solution)/shard_map/all_to_all | solution.py:77
  1345.6 91.7 %all-reduce.5.cloned.1.call-start = ((), (), s32[]{:S(2)}) async-start(), calls=%async_computation.7 | async-start | bytes 524288 | tf_op jit(solution)/shard_map/psum | solution.py:87
Sparse Core Ops, SparseCore 0:
  557.7 24.6 all-reduce.2
  1412.1 25.1 all-reduce.4
where the time goes:
time: 2160 us
  blocking collectives  1760 us (81%)
  waiting for transfers between devices  132 us (6%)
  local copies, waits for them, and re-layouts  90.2 us (4%)
  other arithmetic  81.1 us (4%)
  starting transfers between devices  63.8 us (3%)
    psum x2, blocking collectives, local(): gram = lax.psum(inner(residual, residual), 'rows')  709 us
    psum x2, blocking collectives, local(): alpha = lax.psum(inner(current, applied), 'rows')  696 us
    psum x1, blocking collectives, local(): first = lax.psum(inner(full_start, full_start), 'rows')  348 us
    all_to_all x2, waiting for transfers between devices, local(): lax.all_to_all(outgoing.reshape(groups, capacity, width_k * cluster), 'ro...  65.7 us
    scatter-add x2, other arithmetic, local(): summed = forward.at[asked].add(returned)  62.2 us
    psum x2, waiting for transfers between devices, local(): product = lax.psum(product, 'sub')  50.1 us
  transfers between devices with their start and end apart: 8, of which 6 were waited for; matrix products, arithmetic and copies ran while one was open for 3% of the time, Pallas kernels for 0%

commit v1 on v0

v1 whole, which is shorter than its diff:
```python
import math

import jax
import jax.numpy as jnp
from jax import lax
from jax.experimental import pallas as pl
from jax.experimental.pallas import tpu as pltpu
from jax.sharding import PartitionSpec as P

STEPS = 2
MESH = pl.DeviceIdType.MESH
VMEM = pl.BlockSpec(memory_space=pltpu.VMEM)


def inner(left, right):
    return jnp.dot(left, right.T, precision=lax.Precision.HIGHEST)


def times(left, right):
    return jnp.dot(left, right, precision=lax.Precision.HIGHEST)


def exchange_kernel(in_ref, out_ref, send_sem, recv_sem, local_sem):
    groups = in_ref.shape[0]
    me, sub = lax.axis_index("rows"), lax.axis_index("sub")
    barrier = pltpu.get_barrier_semaphore()

    def greet(i, carry):
        peer = lax.rem(me + i, groups)
        pl.semaphore_signal(barrier, inc=1, device_id=(peer, sub), device_id_type=MESH)
        return carry

    lax.fori_loop(1, groups, greet, 0)
    own = pltpu.make_async_copy(in_ref.at[me], out_ref.at[me], local_sem)
    own.start()
    pl.semaphore_wait(barrier, groups - 1)

    def send(i, carry):
        peer = lax.rem(me + i, groups)
        pltpu.make_async_remote_copy(
            src_ref=in_ref.at[peer],
            dst_ref=out_ref.at[me],
            send_sem=send_sem,
            recv_sem=recv_sem,
            device_id=(peer, sub),
            device_id_type=MESH,
        ).start()
        return carry

    lax.fori_loop(1, groups, send, 0)
    own.wait()
    rest = pl.ds(0, groups - 1)
    pltpu.make_async_remote_copy(
        src_ref=in_ref.at[rest],
        dst_ref=out_ref.at[rest],
        send_sem=send_sem,
        recv_sem=recv_sem,
        device_id=(lax.rem(me + 1, groups), sub),
        device_id_type=MESH,
    ).wait()


def exchange(x, ident):
    return pl.pallas_call(
        exchange_kernel,
        out_shape=jax.ShapeDtypeStruct(x.shape, x.dtype),
        in_specs=[VMEM],
        out_specs=VMEM,
        scratch_shapes=[pltpu.SemaphoreType.DMA] * 3,
        compiler_params=pltpu.CompilerParams(
            collective_id=ident, has_side_effects=True, vmem_limit_bytes=32 << 20
        ),
    )(x)


def total_kernel(sizes, x_ref, o_ref, near, far, send_sem, recv_sem):
    nx, nz, ny = sizes
    me, sub = lax.axis_index("rows"), lax.axis_index("sub")
    x, z, y = me // (nz * ny), lax.rem(me // ny, nz), lax.rem(me, ny)

    def device(x, z, y):
        return ((lax.rem(x, nx) * nz + lax.rem(z, nz)) * ny + lax.rem(y, ny), sub)

    plane = [device(x + a, z, y + b) for a in range(nx) for b in range(ny)][1:]
    line = [device(x, z + a, y) for a in range(1, nz)]
    barrier = pltpu.get_barrier_semaphore()
    for peer in plane + line:
        pl.semaphore_signal(barrier, inc=1, device_id=peer, device_id_type=MESH)
    pl.semaphore_wait(barrier, len(plane) + len(line))
    current = x_ref[...]
    for k, (slots, place, peers) in enumerate(((near, x * ny + y, plane), (far, z, line))):
        slots[pl.ds(place, 1)] = current[None]
        for peer in peers:
            pltpu.make_async_remote_copy(
                src_ref=slots.at[place],
                dst_ref=slots.at[place],
                send_sem=send_sem.at[k],
                recv_sem=recv_sem.at[k],
                device_id=peer,
                device_id_type=MESH,
            ).start()
        others = pl.ds(0, len(peers))
        pltpu.make_async_remote_copy(
            src_ref=slots.at[others],
            dst_ref=slots.at[others],
            send_sem=send_sem.at[k],
            recv_sem=recv_sem.at[k],
            device_id=peers[0],
            device_id_type=MESH,
        ).wait()
        current = jnp.sum(slots[...], axis=0)
    o_ref[...] = current


def total(x, ident):
    k = x.shape[0]
    padded = jnp.pad(x, ((0, 0), (0, 128 - k)))
    out = pl.pallas_call(
        lambda *refs: total_kernel((4, 8, 4), *refs),
        out_shape=jax.ShapeDtypeStruct(padded.shape, x.dtype),
        in_specs=[VMEM],
        out_specs=VMEM,
        scratch_shapes=[
            pltpu.VMEM((16,) + padded.shape, x.dtype),
            pltpu.VMEM((8,) + padded.shape, x.dtype),
            pltpu.SemaphoreType.DMA((2,)),
            pltpu.SemaphoreType.DMA((2,)),
        ],
        compiler_params=pltpu.CompilerParams(collective_id=ident, has_side_effects=True),
    )(padded)
    return out[:, :k]


def local(upper_tiles, tile_clusters, cluster_slot, start_block):
    blocks = upper_tiles.shape[0]
    cluster = upper_tiles.shape[1]
    groups = lax.axis_size("rows")
    capacity = 2 * blocks // groups + 2
    per_row = upper_tiles.shape[2] // cluster
    stacked = upper_tiles.reshape(blocks, cluster, per_row, cluster).transpose(0, 2, 1, 3)
    targets = cluster_slot[tile_clusters].reshape(-1)
    owners = targets // blocks
    local_block = targets % blocks
    count = owners.shape[0]
    order = jnp.arange(count, dtype=jnp.int32)
    before = (owners[:, None] == owners[None, :]) & (order[None, :] < order[:, None])
    ranks = jnp.sum(before.astype(jnp.int32), axis=1)
    slots = owners * capacity + ranks
    tile_columns = jnp.sum(stacked, axis=2, dtype=jnp.float32).reshape(count, cluster)
    named = jnp.concatenate([tile_columns, local_block.astype(jnp.float32)[:, None]], axis=1)
    named = jnp.pad(named, ((0, 0), (0, 128 - cluster - 1)))
    column_out = jnp.zeros((groups * capacity, 128), jnp.float32).at[slots].set(named)
    column_back = exchange(column_out.reshape(groups, capacity, 128), 1)
    column_back = column_back.reshape(groups * capacity, 128)
    asked = column_back[:, cluster].astype(jnp.int32)
    own_degree = jnp.sum(stacked, axis=(1, 3), dtype=jnp.float32)
    degree = own_degree.at[asked].add(column_back[:, :cluster])
    degree = lax.psum(degree, "sub")
    scale = lax.rsqrt(degree.reshape(blocks * cluster))
    full_start = lax.all_gather(start_block, "sub", axis=0, tiled=True)
    first = total(inner(full_start, full_start), 4)
    lower = jnp.linalg.cholesky(first)
    current = lax.linalg.triangular_solve(lower, full_start, left_side=True, lower=True)
    previous = jnp.zeros_like(current)
    link = jnp.zeros_like(first)
    nodes = blocks * cluster * groups
    half_rows = start_block.shape[0]
    bases = []
    coeffs = []
    for step in range(STEPS):
        width_k = current.shape[0]
        scaled = (current * scale[None, :]).astype(jnp.bfloat16)
        scaled = scaled.reshape(width_k, blocks, cluster).transpose(1, 0, 2)
        reply = scaled[asked].reshape(groups, capacity * width_k * cluster // 128, 128)
        mirrored = jnp.einsum("bkr,bwrc->bwkc", scaled, stacked, preferred_element_type=jnp.float32)
        mirrored = mirrored.reshape(count, width_k, cluster)
        outgoing = (
            jnp.zeros((groups * capacity, width_k, cluster), jnp.float32).at[slots].set(mirrored)
        )
        outgoing = outgoing.astype(jnp.bfloat16).reshape(reply.shape)
        both = exchange(jnp.concatenate([reply, outgoing], axis=1), 2)
        fetched, returned = jnp.split(both, 2, axis=1)
        fetched = fetched.reshape(groups * capacity, width_k, cluster)
        returned = returned.reshape(groups * capacity, width_k, cluster).astype(jnp.float32)
        partner = fetched[slots].reshape(blocks, per_row, width_k, cluster)
        forward = jnp.einsum("bwkc,bwrc->bkr", partner, stacked, preferred_element_type=jnp.float32)
        summed = forward.at[asked].add(returned)
        product = summed.transpose(1, 0, 2).reshape(width_k, blocks * cluster)
        product = lax.psum(product, "sub")
        applied = current - scale[None, :] * product
        alpha = total(inner(current, applied), 4)
        residual = applied - times(alpha.T, current) - times(link.T, previous)
        gram = total(inner(residual, residual), 4)
        lower = jnp.linalg.cholesky(gram)
        following = lax.linalg.triangular_solve(lower, residual, left_side=True, lower=True)
        coeffs.append(alpha)
        coeffs.append(lower.T)
        own_rows = lax.dynamic_slice_in_dim(
            following, lax.axis_index("sub") * half_rows, half_rows, 0
        )
        bases.append(own_rows * math.sqrt(nodes))
        previous, current, link = (current, following, lower)
    return (jnp.stack(bases), jnp.stack(coeffs))


def solution(mesh):
    in_specs = (P("rows", None, "sub"), P("rows", "sub"), P(), P("sub", "rows"))
    out_specs = (P(None, "sub", "rows"), P())
    return jax.shard_map(local, mesh=mesh, in_specs=in_specs, out_specs=out_specs, check_vma=False)
```

time: 2160 us -> 459 us (0.21)
  blocking collectives: 1760 us -> 5.57 us
  Pallas kernels: 0 us -> 186 us
  waiting for transfers between devices: 132 us -> 54.5 us
  starting transfers between devices: 63.8 us -> 0.3 us
    psum x5 -> x0, blocking collectives: 1750 us -> none  [the longest x2 709 us: local(): gram = lax.psum(inner(residual, residual), 'rows')]
    pallas_call x0 -> x8, Pallas kernels: none -> 186 us  [the longest x3 103 us: exchange(): pl.pallas_call(exchange_kernel, out_shape=jax.ShapeDtypeStruct(x.shape, x...]
    all_to_all x6 -> x0, waiting for transfers between devices: 82.3 us -> none  [the longest x2 65.7 us: local(): lax.all_to_all(outgoing.reshape(groups, capacity, width_k * cluster), 'ro...]
    all_to_all x6 -> x0, starting transfers between devices: 63.7 us -> none  [the longest x2 22.5 us: local(): lax.all_to_all(outgoing.reshape(groups, capacity, width_k * cluster), 'ro...]
  transfers between devices with their start and end apart: 8 -> 2, of which waited for: 6 -> 2; matrix products, arithmetic and copies ran while one was open for 3% -> 0% of each run, Pallas kernels for 0% -> 0%
where the time goes in v1:
time: 459 us; the launch traced here: 456 us
  Pallas kernels  186 us (41%)
  other arithmetic  94.8 us (21%)
  local copies, waits for them, and re-layouts  86.1 us (19%)
  waiting for transfers between devices  54.5 us (12%)
  matrix products  14.7 us (3%)
  between operations  14.5 us (3%)
  blocking collectives  5.57 us (1%)
    pallas_call x3, Pallas kernels, exchange(): pl.pallas_call(exchange_kernel, out_shape=jax.ShapeDtypeStruct(x.shape, x...  103 us
    pallas_call x5, Pallas kernels, total(): pl.pallas_call(lambda *refs: total_kernel((4, 8, 4), *refs), out_shape=ja...  83.2 us
    scatter-add x2, other arithmetic, local(): summed = forward.at[asked].add(returned)  62.3 us
    psum x2, waiting for transfers between devices, local(): product = lax.psum(product, 'sub')  54.5 us
    scatter x2, local copies, waits for them, and re-layouts, local(): jnp.zeros((groups * capacity, width_k, cluster), jnp.float32).at[slots]  30.8 us
  transfers between devices with their start and end apart: 2, of which 2 were waited for; matrix products, arithmetic and copies ran while one was open for 0% of the time, Pallas kernels for 0%

profile of v1, /device:TPU:8, one launch (start us, length us, event | category | flops | bytes accessed | tf_op | source)
XLA Modules:
  0.0 456.4 jit_solution(7030287622839248112)
XLA Ops:
  7.2 3.9 reshape.248
  14.8 19.4 %shard_map.60 = f32[128,3,128]{2,1,0:T(4,128)S(1)} custom-call(f32[128,3,128]{2,1,0:T(4,128)S(1)} %reshape.252.in_ref), custom_call_target="tpu_custom_call" | custom-call | tf_op jit(solution)/shard_map/pallas_call | solution.py:64
  34.5 2.7 scatter_custom_fusion.1
  37.2 3.4 psum.21
  40.7 2.2 all_gather.3
  44.0 15.6 %shard_map.59 = f32[16,128]{1,0:T(8,128)} custom-call(f32[16,128]{1,0:T(8,128)} %pad.20.refs_0_), custom_call_target="tpu_custom_call" | custom-call | tf_op jit(solution)/shard_map/pallas_call | solution.py:118
  61.1 1.4 cholesky.59
  65.8 1.4 fusion.6
  67.4 1.9 broadcast.216.clone
  69.3 15.4 %scatter_fusion = f32[384,16,64]{2,1,0:T(8,128)} fusion(f32[384,16,64]{2,1,0:T(8,128)} %broadcast.216.clone, s32[128]{0:T(128)S(1)} %get-tuple-element.21, f32[128,16,64]{2,1,0:T(8,128)} %bitcast.143), kind=kCustom, calls=%fused_computation.7 | custom fusion | bytes 1573376 | tf_op jit(solution)/shard_map/scatter | solution.py:178
  84.7 3.2 convert_element_type.58
  87.9 3.4 reshape.257
  91.3 2.6 gather_fusion.1
  93.8 3.3 reshape.255
  97.2 1.5 pad_maximum_fusion.in_ref
  98.7 42.4 %shard_map.61 = bf16[128,48,128]{2,1,0:T(8,128)(2,1)S(1)} custom-call(bf16[128,48,128]{2,1,0:T(8,128)(2,1)S(1)} %pad_maximum_fusion.in_ref), custom_call_target="tpu_custom_call" | custom-call | tf_op jit(solution)/shard_map/pallas_call | solution.py:64
  141.2 1.6 slice_convert_fusion.1
  142.8 3.2 reshape.258
  146.0 2.1 gather_fusion.2
  148.7 3.4 reshape.342
  152.1 31.1 %scatter_fusion.1 = f32[64,16,64]{2,1,0:T(8,128)S(1)} fusion(f32[64,16,64]{2,1,0:T(8,128)S(1)} %fusion.8, s32[384]{0:T(512)S(1)} %fusion.24, f32[384,16,64]{2,1,0:T(8,128)} %reshape.342), kind=kCustom, calls=%fused_computation.8 | custom fusion | flops 393216 | bytes 4720128 | tf_op jit(solution)/shard_map/scatter-add | solution.py:187
  184.6 27.8 %all-reduce.9.cloned.1.call-done = f32[16,4096]{1,0:T(8,128)} async-done(((f32[16,4096]{1,0:T(8,128)}), f32[16,4096]{1,0:T(8,128)}) %all-reduce.9.cloned.1.call-update) | async-done | bytes 262160 | tf_op jit(solution)/shard_map/psum | solution.py:189
  212.4 1.4 fusion.21
  214.4 17.7 %shard_map.62 = f32[16,128]{1,0:T(8,128)} custom-call(f32[16,128]{1,0:T(8,128)} %pad.22.refs_0_), custom_call_target="tpu_custom_call" | custom-call | tf_op jit(solution)/shard_map/pallas_call | solution.py:118
  232.1 1.4 convolution_subtract_fusion.3
  234.9 16.0 %shard_map.63 = f32[16,128]{1,0:T(8,128)} custom-call(f32[16,128]{1,0:T(8,128)} %pad.23.refs_0_), custom_call_target="tpu_custom_call" | custom-call | tf_op jit(solution)/shard_map/pallas_call | solution.py:118
  252.4 1.4 cholesky.70
  257.1 1.4 fusion.2
  258.7 1.9 broadcast.216
  260.6 15.4 %scatter_fusion.2 = f32[384,16,64]{2,1,0:T(8,128)} fusion(f32[384,16,64]{2,1,0:T(8,128)} %broadcast.216, s32[128]{0:T(128)S(1)} %get-tuple-element.21, f32[128,16,64]{2,1,0:T(8,128)} %bitcast.144), kind=kCustom, calls=%fused_computation.9 | custom fusion | bytes 1573376 | tf_op jit(solution)/shard_map/scatter | solution.py:178
  276.0 3.2 convert_element_type.62
  279.2 3.4 reshape.264
  282.6 2.6 gather_fusion.3
  285.2 3.3 reshape.262
  288.5 1.5 pad_maximum_fusion.1.in_ref
  290.0 41.0 %shard_map.64 = bf16[128,48,128]{2,1,0:T(8,128)(2,1)S(1)} custom-call(bf16[128,48,128]{2,1,0:T(8,128)(2,1)S(1)} %pad_maximum_fusion.1.in_ref), custom_call_target="tpu_custom_call" | custom-call | tf_op jit(solution)/shard_map/pallas_call | solution.py:64
  331.0 1.6 slice_convert_fusion
  332.6 3.2 reshape.265
  335.8 2.9 gather_fusion.4
  338.7 1.7 fusion.11
  340.4 3.4 reshape.358
  343.7 31.1 %scatter_fusion.3 = f32[64,16,64]{2,1,0:T(8,128)S(1)} fusion(f32[64,16,64]{2,1,0:T(8,128)S(1)} %fusion.11, s32[384]{0:T(512)S(1)} %fusion.24, f32[384,16,64]{2,1,0:T(8,128)} %reshape.358), kind=kCustom, calls=%fused_computation.10 | custom fusion | flops 393216 | bytes 4720128 | tf_op jit(solution)/shard_map/scatter-add | solution.py:187
  376.1 26.7 %all-reduce.11.cloned.1.call-done = f32[16,4096]{1,0:T(8,128)} async-done(((f32[16,4096]{1,0:T(8,128)}), f32[16,4096]{1,0:T(8,128)}) %all-reduce.11.cloned.1.call-update) | async-done | bytes 262160 | tf_op jit(solution)/shard_map/psum | solution.py:189
  402.8 1.4 fusion.20
  404.8 17.7 %shard_map.65 = f32[16,128]{1,0:T(8,128)} custom-call(f32[16,128]{1,0:T(8,128)} %pad.24.refs_0_), custom_call_target="tpu_custom_call" | custom-call | tf_op jit(solution)/shard_map/pallas_call | solution.py:118
  422.5 1.4 convolution_subtract_fusion.1
  426.1 16.1 %shard_map.66 = f32[16,128]{1,0:T(8,128)} custom-call(f32[16,128]{1,0:T(8,128)} %pad.25.refs_0_), custom_call_target="tpu_custom_call" | custom-call | tf_op jit(solution)/shard_map/pallas_call | solution.py:118
  443.6 1.4 cholesky.81
  (78 shorter events, 28.8 us)
Async XLA Ops:
  7.2 5.0 %copy-start = (s32[8192]{0:T(1024)S(1)}, s32[8192]{0:T(1024)}, u32[]{:S(2)}) copy-start(s32[8192]{0:T(1024)} %param.9) | copy-start | bytes 98308
  7.2 4.7 %copy-start.4 = (s32[64,2]{0,1:T(2,128)S(1)}, s32[64,2]{0,1:T(2,128)}, u32[]{:S(2)}) copy-start(s32[64,2]{0,1:T(2,128)} %param.8) | copy-start | bytes 1540
  7.2 205.2 %all-reduce.9.cloned.1.call-start = ((), (), s32[]{:S(2)}) async-start(), calls=%async_computation | async-start | bytes 524288 | tf_op jit(solution)/shard_map/psum | solution.py:189
  13.4 27.4 %copy-start.1 = (f32[8,4096]{1,0:T(8,128)S(1)}, f32[8,4096]{1,0:T(8,128)}, u32[]{:S(2)}) copy-start(f32[8,4096]{1,0:T(8,128)} %param.10) | copy-start | bytes 393220
  184.3 218.4 %all-reduce.11.cloned.1.call-start = ((), (), s32[]{:S(2)}) async-start(), calls=%async_computation.1 | async-start | bytes 524288 | tf_op jit(solution)/shard_map/psum | solution.py:189
  374.9 1.1 copy-start.2
  422.5 25.5 %copy-start.3 = (f32[16,128]{1,0:T(8,128)S(1)}, f32[16,128]{1,0:T(8,128)}, u32[]{:S(2)}) copy-start(f32[16,128]{1,0:T(8,128)} %shard_map.65) | copy-start | bytes 24580
Sparse Core Ops, SparseCore 0:
  184.4 27.8 all-reduce.8
  376.1 26.6 all-reduce.10

commit v2 on v0

v2 whole, which is shorter than its diff:
```python
import functools
import math

import jax
import jax.numpy as jnp
from jax import lax
from jax.experimental import pallas as pl
from jax.experimental.pallas import tpu as pltpu
from jax.sharding import PartitionSpec as P

CAP = 3
MESH = pl.DeviceIdType.MESH
VMEM = pl.BlockSpec(memory_space=pltpu.VMEM)
SMEM = pl.BlockSpec(memory_space=pltpu.SMEM)
F32 = jnp.float32
BF16 = jnp.bfloat16
LIMIT = 40 << 20
EXACT = lax.Precision.HIGHEST


def dot(left, right):
    return jnp.dot(left, right, precision=EXACT, preferred_element_type=F32)


def dot_t(left, right):
    dims = (((1,), (1,)), ((), ()))
    return lax.dot_general(left, right, dims, precision=EXACT, preferred_element_type=F32)


def swap(x):
    return pltpu.roll(x, 64, 1)


def is_low(shape):
    return lax.broadcasted_iota(jnp.int32, shape, 1) < 64


def pair_up(first, second):
    low = is_low(first.shape)
    return jnp.where(low, first, swap(second)), jnp.where(low, swap(first), second)


class Place:
    def __init__(self, sizes):
        self.nx, self.nz, self.ny = sizes
        self.groups = self.nx * self.nz * self.ny
        self.me, self.sub = lax.axis_index("rows"), lax.axis_index("sub")
        self.x = self.me // (self.nz * self.ny)
        self.z = lax.rem(self.me // self.ny, self.nz)
        self.y = lax.rem(self.me, self.ny)
        self.other = (self.me, 1 - self.sub)
        nx, nz, ny = sizes
        self.plane = [self.at(a, 0, b, 0) for a in range(nx) for b in range(ny)][1:]
        self.line = [self.at(0, a, 0, s) for a in range(nz) for s in range(2)][1:]
        self.slots = (self.x * ny + self.y, self.z * 2 + self.sub)

    def at(self, dx, dz, dy, ds):
        x, z, y = lax.rem(self.x + dx, self.nx), lax.rem(self.z + dz, self.nz), lax.rem(self.y + dy, self.ny)
        return ((x * self.nz + z) * self.ny + y, lax.rem(self.sub + ds, 2))

    def peer(self, i):
        return (lax.rem(self.me + i, self.groups), self.sub)


def signal(barrier, device):
    pl.semaphore_signal(barrier, inc=1, device_id=device, device_id_type=MESH)


def meet(place, everyone):
    barrier = pltpu.get_barrier_semaphore()
    if everyone:
        def greet(i, carry):
            signal(barrier, place.peer(i))
            return carry

        lax.fori_loop(1, place.groups, greet, 0, unroll=8)
        rest = [d for k, d in enumerate(place.line) if k % 2 == 0]
        count = place.groups - 1 + len(rest)
    else:
        rest = place.plane + place.line
        count = len(rest)
    for device in rest:
        signal(barrier, device)
    return lambda: pl.semaphore_wait(barrier, count)


def remote(src, dst, send_sem, recv_sem, device):
    return pltpu.make_async_remote_copy(
        src_ref=src, dst_ref=dst, send_sem=send_sem, recv_sem=recv_sem, device_id=device, device_id_type=MESH
    )


def total(place, current, near, far, send_sem, recv_sem):
    for k, (held, slot, peers) in enumerate(
        ((near, place.slots[0], place.plane), (far, place.slots[1], place.line))
    ):
        held[pl.ds(slot, 1)] = current[None]
        for device in peers:
            remote(held.at[slot], held.at[slot], send_sem.at[k], recv_sem.at[k], device).start()
        rest = pl.ds(0, len(peers))
        remote(held.at[rest], held.at[rest], send_sem.at[k], recv_sem.at[k], peers[0]).wait()
        current = jnp.sum(held[...], axis=0)
    return current


def total_scratch(sizes):
    nx, nz, ny = sizes
    return [
        pltpu.VMEM((nx * ny, 16, 128), F32),
        pltpu.VMEM((nz * 2, 16, 128), F32),
        pltpu.SemaphoreType.DMA((2,)),
        pltpu.SemaphoreType.DMA((2,)),
    ]


def send_all(place, build, src, dst, send_sem, recv_sem, own_sem):
    me, groups = place.me, place.groups
    build(me)
    own = pltpu.make_async_copy(src.at[me], dst.at[me], own_sem)
    own.start()

    def send(i, carry):
        peer, sub = place.peer(i)
        build(peer)
        remote(src.at[peer], dst.at[me], send_sem, recv_sem, (peer, sub)).start()
        return carry

    lax.fori_loop(1, groups, send, 0, unroll=2)
    rest = pl.ds(0, groups - 1)

    def finish():
        own.wait()
        remote(src.at[rest], dst.at[rest], send_sem, recv_sem, place.peer(1)).wait()

    return finish


def factor(gram):
    n = gram.shape[0]
    row = lax.broadcasted_iota(jnp.int32, (n, n), 0)
    col = lax.broadcasted_iota(jnp.int32, (n, n), 1)
    left = gram
    right = jnp.where(row == col, 1.0, 0.0).astype(F32)
    below = lax.broadcasted_iota(jnp.int32, (n, 1), 0)
    for i in range(n):
        share = jnp.where(below > i, left[:, i : i + 1] / left[i : i + 1, i : i + 1], 0.0)
        right = right - share * right[i : i + 1, :]
        left = left - share * left[i : i + 1, :]
    pivots = jnp.sum(jnp.where(row == col, left, 0.0), axis=1, keepdims=True)
    root = lax.rsqrt(pivots)
    return jnp.where(col >= row, left * root, 0.0), right * root


def widen(x):
    return jnp.concatenate([x, jnp.zeros((x.shape[0], 128 - x.shape[1]), F32)], axis=1)


def prepare_blocks(vectors, scale, tiles, scaled, mirrored, blocks):
    scaled[blocks] = jnp.zeros((8, 128), F32)
    mirrored[2 * blocks] = jnp.zeros((8, 128), F32)

    def step(t, carry):
        lanes = pl.ds(pl.multiple_of(t * 128, 128), 128)
        halves = pair_up(vectors[0:8, lanes], vectors[8:16, lanes])
        for p in range(2):
            b = 2 * t + p
            block = halves[p] * jnp.broadcast_to(scale[pl.ds(b, 1), :], (8, 128))
            scaled[b] = block
            left = jnp.concatenate([block, swap(block)], axis=0)[:, :64].astype(BF16)
            out = jnp.dot(left, tiles[b], preferred_element_type=F32)
            first, second = pair_up(out[0:8], out[8:16])
            mirrored[2 * b] = first
            mirrored[2 * b + 1] = second
        return carry

    lax.fori_loop(0, blocks // 2, step, 0, unroll=4)


def chunk_builder(asked, placed, scaled, mirrored, chunks):
    def build(d):
        parts = [scaled[asked[CAP * d + k]] for k in range(CAP)]
        parts += [mirrored[placed[CAP * d + k]] for k in range(CAP)]
        chunks[d] = jnp.concatenate(parts, axis=0).astype(BF16)

    return build


def open_kernel(
    sizes, blocks, tiles, start, names, placed, received, full, first, own_degree,
    named, chunks, near, far, tsend, trecv, send_sem, recv_sem, own_sem, xsend, xrecv, xown,
):
    place = Place(sizes)
    ready = meet(place, True)
    rows = pl.ds(pl.multiple_of(place.sub * 8, 8), 8)
    keep = pltpu.make_async_copy(start, full.at[rows], xown)
    keep.start()
    named[2 * blocks] = jnp.broadcast_to(names[pl.ds(2 * blocks, 1), :], (8, 128))

    def sums(b, carry):
        tile = tiles[b]
        columns = jnp.dot(jnp.ones((8, 64), BF16), tile, preferred_element_type=F32)
        low = is_low(columns.shape)
        named[2 * b] = jnp.where(low, columns, names[pl.ds(2 * b, 1), :])
        named[2 * b + 1] = jnp.where(low, swap(columns), names[pl.ds(2 * b + 1, 1), :])
        dims = (((1,), (1,)), ((), ()))
        across = lax.dot_general(jnp.ones((8, 128), BF16), tile, dims, preferred_element_type=F32)
        own_degree[pl.ds(b, 1), :] = jnp.concatenate([across, across], axis=1)[0:1]
        return carry

    lax.fori_loop(0, blocks, sums, 0, unroll=4)
    ready()
    swap_rows = remote(start, full.at[rows], xsend, xrecv, place.other)
    swap_rows.start()

    def build(d):
        for k in range(CAP):
            chunks[d, pl.ds(k, 1), :] = named[placed[CAP * d + k]][0:1]

    finish = send_all(place, build, chunks, received, send_sem, recv_sem, own_sem)
    keep.wait()
    swap_rows.wait()
    half = full.shape[1] // 2
    part = full[:, pl.ds(pl.multiple_of(place.sub * half, 128), half)]
    first[...] = total(place, widen(dot_t(part, part)), near, far, tsend, trecv)
    finish()


def degree_kernel(blocks, received, asked, own_degree, degree, acc0, acc1, acc2):
    accs = (acc0, acc1, acc2)
    for acc in accs:
        acc[...] = jnp.zeros_like(acc)

    def add(d, carry):
        rows = received[d]
        for k in range(CAP):
            i = asked[CAP * d + k]
            accs[k][i] = accs[k][i] + jnp.broadcast_to(rows[k : k + 1, :], (8, 128))
        return carry

    lax.fori_loop(0, received.shape[0], add, 0, unroll=4)

    def gather(b, carry):
        summed = acc0[b] + acc1[b] + acc2[b]
        summed = jnp.where(is_low(summed.shape), summed, swap(summed))
        degree[pl.ds(b, 1), :] = own_degree[pl.ds(b, 1), :] + summed[0:1]
        return carry

    lax.fori_loop(0, blocks, gather, 0, unroll=4)


def first_kernel(
    sizes, blocks, tiles, degree, full, first, asked, placed, received, vectors, scale,
    theirs, scaled, mirrored, chunks, send_sem, recv_sem, own_sem, xsend, xrecv,
):
    place = Place(sizes)
    ready = meet(place, True)
    _, inverse = factor(first[:, :16])
    vectors[...] = dot(inverse, full[...])
    ready()
    pair = remote(degree, theirs, xsend, xrecv, place.other)
    pair.start()
    pair.wait()
    scale[...] = lax.rsqrt(degree[...] + theirs[...])
    prepare_blocks(vectors, scale, tiles, scaled, mirrored, blocks)
    build = chunk_builder(asked, placed, scaled, mirrored, chunks)
    send_all(place, build, chunks, received, send_sem, recv_sem, own_sem)()


def apply_kernel(blocks, tiles, received, where, asked, product, held, acc0, acc1, acc2):
    accs = (acc0, acc1, acc2)
    for acc in accs:
        acc[...] = jnp.zeros_like(acc)

    def spread(d, carry):
        chunk = received[d].astype(F32).reshape(2 * CAP, 8, 128)
        held[pl.ds(d * CAP, CAP)] = chunk[:CAP]
        for k in range(CAP):
            i = asked[CAP * d + k]
            accs[k][i] = accs[k][i] + chunk[CAP + k]
        return carry

    lax.fori_loop(0, received.shape[0], spread, 0, unroll=4)

    def forward(b, carry):
        low, high = pair_up(held[where[2 * b]], held[where[2 * b + 1]])
        left = jnp.concatenate([low, high], axis=0).astype(BF16)
        dims = (((1,), (1,)), ((), ()))
        out = lax.dot_general(left, tiles[b], dims, preferred_element_type=F32)
        out = jnp.concatenate([out[0:8], out[8:16]], axis=1)
        product[b] = out + acc0[b] + acc1[b] + acc2[b]
        return carry

    lax.fori_loop(0, blocks, forward, 0, unroll=4)


def step_kernel(sizes, blocks, nodes, last, *refs):
    refs = list(refs)
    product, scale, current, previous, link = refs[:5]
    del refs[:5]
    if not last:
        tiles, asked, placed, received, vectors = refs[:5]
        del refs[:5]
    basis, alpha_out, upper_out = refs[:3]
    theirs, stack, near, far, tsend, trecv, xsend, xrecv = refs[3:11]
    del refs[:11]
    if last:
        (vectors,) = refs
    else:
        scaled, mirrored, chunks, send_sem, recv_sem, own_sem = refs
    place = Place(sizes)
    ready = meet(place, not last)
    stack[16:32] = current[...]
    stack[32:48] = previous[...]
    ready()
    pair = remote(product, theirs, xsend, xrecv, place.other)
    pair.start()
    pair.wait()

    def residual(t, carry):
        lanes = pl.ds(pl.multiple_of(t * 128, 128), 128)
        both = []
        for p in range(2):
            b = 2 * t + p
            both.append((product[b] + theirs[b]) * jnp.broadcast_to(scale[pl.ds(b, 1), :], (8, 128)))
        low, high = pair_up(both[0], both[1])
        stack[0:8, lanes] = low
        stack[8:16, lanes] = high
        return carry

    lax.fori_loop(0, blocks // 2, residual, 0, unroll=4)
    half = current.shape[1] // 2
    part = stack[:, pl.ds(pl.multiple_of(place.sub * half, 128), half)]
    gram = dot_t(part, part)
    packed = widen(jnp.concatenate([gram[0:16], gram[16:32], gram[32:48, 32:48]], axis=1))
    packed = total(place, packed, near, far, tsend, trecv)
    rr, rq, rp, qr, qq, qp, pp = (packed[:, 16 * k : 16 * k + 16] for k in range(7))
    gram = jnp.concatenate(
        [
            jnp.concatenate([rr, rq, rp], axis=1),
            jnp.concatenate([qr, qq, qp], axis=1),
            jnp.concatenate([rp.T, qp.T, pp], axis=1),
        ],
        axis=0,
    )
    alpha = qq - qr
    row = lax.broadcasted_iota(jnp.int32, (16, 16), 0)
    col = lax.broadcasted_iota(jnp.int32, (16, 16), 1)
    eye = jnp.where(row == col, 1.0, 0.0).astype(F32)
    mix = jnp.concatenate([-eye, eye - alpha.T, -link[:, :16]], axis=1)
    upper, inverse = factor(dot_t(dot(mix, gram), mix))
    vectors[...] = dot(dot(inverse, mix), stack[...])
    alpha_out[...] = widen(alpha)
    upper_out[...] = widen(upper)
    rows = pl.ds(pl.multiple_of(place.sub * 8, 8), 8)
    basis[...] = vectors[rows, :] * math.sqrt(nodes)
    if not last:
        prepare_blocks(vectors, scale, tiles, scaled, mirrored, blocks)
        build = chunk_builder(asked, placed, scaled, mirrored, chunks)
        send_all(place, build, chunks, received, send_sem, recv_sem, own_sem)()


def call(kernel, name, ident, outs, scratch, specs, *args):
    params = {"vmem_limit_bytes": LIMIT}
    if ident is not None:
        params |= {"collective_id": ident, "has_side_effects": True}
    return pl.pallas_call(
        kernel,
        out_shape=[jax.ShapeDtypeStruct(*o) for o in outs],
        in_specs=specs,
        out_specs=[VMEM] * len(outs),
        scratch_shapes=scratch,
        compiler_params=pltpu.CompilerParams(**params),
        name=name,
    )(*args)


def local(sizes, upper_tiles, tile_clusters, cluster_slot, start_block):
    blocks, cluster, _ = upper_tiles.shape
    groups = sizes[0] * sizes[1] * sizes[2]
    columns = blocks * cluster
    nodes = columns * groups
    count = 2 * blocks
    targets = cluster_slot[tile_clusters].reshape(-1)
    owners = targets // blocks
    order = jnp.arange(count, dtype=jnp.int32)
    before = (owners[:, None] == owners[None, :]) & (order[None, :] < order[:, None])
    ranks = jnp.sum(before.astype(jnp.int32), axis=1)
    where = owners * CAP + ranks
    placed = jnp.full((groups * CAP,), count, jnp.int32).at[where].set(order)
    ids = jnp.concatenate([targets % blocks, jnp.full((1,), blocks, jnp.int32)])
    names = jnp.broadcast_to(ids.astype(F32)[:, None], (count + 1, 128))

    dma = pltpu.SemaphoreType.DMA
    block = lambda n: pltpu.VMEM((n, 8, 128), F32)
    chunk = (groups, 16 * CAP, 128)
    received, full, first, own_degree = call(
        functools.partial(open_kernel, sizes, blocks), "open", 1,
        [((groups, CAP, 128), F32), ((16, columns), F32), ((16, 128), F32), ((blocks, 128), F32)],
        [block(count + 1), pltpu.VMEM((groups, CAP, 128), F32)] + total_scratch(sizes) + [dma] * 6,
        [VMEM, VMEM, VMEM, SMEM],
        upper_tiles, start_block, names, placed,
    )
    asked = received[:, :, cluster].astype(jnp.int32).reshape(-1)
    (degree,) = call(
        functools.partial(degree_kernel, blocks), "degree", None,
        [((blocks, 128), F32)],
        [block(blocks + 1)] * 3,
        [VMEM, SMEM, VMEM],
        received, asked, own_degree,
    )
    fill = [block(blocks + 1), block(count + 1), pltpu.VMEM(chunk, BF16)]
    received, vectors, scale = call(
        functools.partial(first_kernel, sizes, blocks), "first", 2,
        [(chunk, BF16), ((16, columns), F32), ((blocks, 128), F32)],
        [pltpu.VMEM((blocks, 128), F32)] + fill + [dma] * 5,
        [VMEM, VMEM, VMEM, VMEM, SMEM, SMEM],
        upper_tiles, degree, full, first, asked, placed,
    )
    previous, link = jnp.zeros_like(vectors), jnp.zeros((16, 128), F32)
    bases, coeffs = [], []
    for last in (False, True):
        (product,) = call(
            functools.partial(apply_kernel, blocks), "apply", None,
            [((blocks, 8, 128), F32)],
            [block(groups * CAP)] + [block(blocks + 1)] * 3,
            [VMEM, VMEM, SMEM, SMEM],
            upper_tiles, received, where, asked,
        )
        common = [((8, columns), F32), ((16, 128), F32), ((16, 128), F32)]
        scratch = [block(blocks), pltpu.VMEM((48, columns), F32)] + total_scratch(sizes) + [dma] * 2
        kernel = functools.partial(step_kernel, sizes, blocks, nodes, last)
        args = [product, scale, vectors, previous, link]
        if last:
            basis, alpha, upper = call(
                kernel, "finish", 4, common, scratch + [pltpu.VMEM((16, columns), F32)], [VMEM] * 5, *args
            )
        else:
            received, following, basis, alpha, upper = call(
                kernel, "step", 3,
                [(chunk, BF16), ((16, columns), F32)] + common,
                scratch + fill + [dma] * 3,
                [VMEM] * 6 + [SMEM] * 2,
                *args, upper_tiles, asked, placed,
            )
            previous, vectors, link = vectors, following, upper
        bases.append(basis)
        coeffs += [alpha[:, :16], upper[:, :16]]
    return jnp.stack(bases), jnp.stack(coeffs)


def solution(mesh):
    sizes = (4, 8, 4)
    in_specs = (P("rows", None, "sub"), P("rows", "sub"), P(), P("sub", "rows"))
    out_specs = (P(None, "sub", "rows"), P())
    body = functools.partial(local, sizes)
    return jax.shard_map(body, mesh=mesh, in_specs=in_specs, out_specs=out_specs, check_vma=False)
```

time: 2160 us -> 187 us (0.09)
  blocking collectives: 1760 us -> 0 us
  Pallas kernels: 0 us -> 177 us
  waiting for transfers between devices: 132 us -> 0 us
  local copies, waits for them, and re-layouts: 90.2 us -> 2.69 us
  other arithmetic: 81.1 us -> 4.63 us
  starting transfers between devices: 63.8 us -> 0 us
    psum x6 -> x0, blocking collectives: 1760 us -> none  [the longest x2 709 us: local(): gram = lax.psum(inner(residual, residual), 'rows')]
    pallas_call x0 -> x7, Pallas kernels: none -> 177 us  [call(): pl.pallas_call(kernel, out_shape=[jax.ShapeDtypeStruct(*o) for o in outs]...]
    all_to_all x6 -> x0, waiting for transfers between devices: 82.3 us -> none  [the longest x2 65.7 us: local(): lax.all_to_all(outgoing.reshape(groups, capacity, width_k * cluster), 'ro...]
    scatter-add x3 -> x0, other arithmetic: 64.8 us -> none  [the longest x2 62.2 us: local(): summed = forward.at[asked].add(returned)]
    all_to_all x6 -> x0, starting transfers between devices: 63.7 us -> none  [the longest x2 22.5 us: local(): lax.all_to_all(outgoing.reshape(groups, capacity, width_k * cluster), 'ro...]
    psum x2 -> x0, waiting for transfers between devices: 50.1 us -> none  [local(): product = lax.psum(product, 'sub')]
    reshape x18 -> x0, local copies, waits for them, and re-layouts: 38 us -> none  [the longest x2 9.06 us: local(): returned = returned.reshape(groups * capacity, width_k, cluster)]
    scatter x4 -> x1, local copies, waits for them, and re-layouts: 32.7 us -> 0.98 us  [local(): placed = jnp.full((groups * CAP,), count, jnp.int32).at[where].set(order)]
  transfers between devices with their start and end apart: 8 -> 0, of which waited for: 6 -> 0; matrix products, arithmetic and copies ran while one was open for 3% -> 0% of each run, Pallas kernels for 0% -> 0%
where the time goes in v2:
time: 187 us; the launch traced here: 185 us
  Pallas kernels  177 us (95%)
  other arithmetic  4.63 us (2%)
  local copies, waits for them, and re-layouts  2.69 us (1%)
    pallas_call x7, Pallas kernels, call(): pl.pallas_call(kernel, out_shape=[jax.ShapeDtypeStruct(*o) for o in outs]...  177 us

profile of v2, /device:TPU:8, one launch (start us, length us, event | category | flops | bytes accessed | tf_op | source)
XLA Modules:
  0.0 184.9 jit_solution(3852965514816590458)
XLA Ops:
  0.6 0.0 copy-start
  0.7 0.7 compare_select_fusion
  1.3 0.1 copy.8
  1.4 0.1 reshape.156
  1.6 0.0 copy-done
  1.6 0.0 copy-start.1
  1.6 0.0 copy-start.2
  1.6 1.1 gather_fusion
  2.8 0.2 convert_reduce_fusion.1
  3.0 1.0 scatter_custom_fusion.placed.refs_7_
  4.0 0.1 broadcast_in_dim.11.names
  4.1 0.0 copy-done.1
  4.1 0.0 copy-done.2
  4.1 26.0 %open.1 = (f32[128,3,128]{2,1,0:T(4,128)S(1)}, f32[16,4096]{1,0:T(8,128)S(1)}, f32[16,128]{1,0:T(8,128)S(1)}, f32[64,128]{1,0:T(8,128)S(1)}) custom-call(bf16[64,64,128]{2,1,0:T(8,128)(2,1)S(1)} %copy-done.1, f32[8,4096]{1,0:T(8,128)S(1)} %copy-done.2, f32[129,128]{1,0:T(8,128)S(1)} %broadcast_in_dim.11.names, s32[384]{0:T(512)S(1)} %scatter_custom_fusion.placed.refs_7_), custom_call_target="tpu_custom_call" | custom-call | tf_op jit(solution)/shard_map/open/pallas_call | solution.py:366
  30.1 2.4 %convert_reduce_fusion = s32[128,3]{1,0:T(8,128)S(1)} fusion(f32[128,3,128]{2,1,0:T(4,128)S(1)} %get-tuple-element.17.received), kind=kLoop, calls=%fused_computation.3 | loop fusion | flops 384 | bytes 3072 | tf_op jit(solution)/shard_map/convert_element_type | solution.py:403
  32.5 0.2 convert_element_type.20.asked.refs_6_
  32.7 2.7 %degree.1 = f32[64,128]{1,0:T(8,128)S(1)} custom-call(f32[128,3,128]{2,1,0:T(4,128)S(1)} %get-tuple-element.17.received, s32[384]{0:T(512)S(1)} %convert_element_type.20.asked.refs_6_, f32[64,128]{1,0:T(8,128)S(1)} %get-tuple-element.18.own_degree), custom_call_target="tpu_custom_call" | custom-call | tf_op jit(solution)/shard_map/degree/pallas_call | solution.py:366
  35.4 48.7 %first.1 = (bf16[128,48,128]{2,1,0:T(8,128)(2,1)S(1)}, f32[16,4096]{1,0:T(8,128)S(1)}, f32[64,128]{1,0:T(8,128)S(1)}) custom-call(bf16[64,64,128]{2,1,0:T(8,128)(2,1)S(1)} %copy-done.1, f32[64,128]{1,0:T(8,128)S(1)} %degree.1, f32[16,4096]{1,0:T(8,128)S(1)} %get-tuple-element.19.full, f32[16,128]{1,0:T(8,128)S(1)} %get-tuple-element.20.first, ...), custom_call_target="tpu_custom_call" | custom-call | tf_op jit(solution)/shard_map/first/pallas_call | solution.py:366
  84.1 6.0 %apply.2.refs_0_ = f32[64,8,128]{2,1,0:T(8,128)S(1)} custom-call(bf16[64,64,128]{2,1,0:T(8,128)(2,1)S(1)} %copy-done.1, bf16[128,48,128]{2,1,0:T(8,128)(2,1)S(1)} %get-tuple-element.21.received, s32[128]{0:T(128)S(1)} %multiply_add_fusion.where, s32[384]{0:T(512)S(1)} %convert_element_type.20.asked.refs_6_), custom_call_target="tpu_custom_call" | custom-call | tf_op jit(solution)/shard_map/apply/pallas_call | solution.py:366
  90.1 65.9 %step.1 = (bf16[128,48,128]{2,1,0:T(8,128)(2,1)S(1)}, f32[16,4096]{1,0:T(8,128)S(1)}, f32[8,4096]{1,0:T(8,128)S(1)}, f32[16,128]{1,0:T(8,128)S(1)}, f32[16,128]{1,0:T(8,128)S(1)}) custom-call(f32[64,8,128]{2,1,0:T(8,128)S(1)} %apply.2.refs_0_, f32[64,128]{1,0:T(8,128)S(1)} %get-tuple-element.22.refs_1_, f32[16,4096]{1,0:T(8,128)S(1)} %get-tuple-element.23.refs_2_.refs_3_, ...), custom_call_target="tpu_custom_call" | custom-call | tf_op jit(solution)/shard_map/step/pallas_call | solution.py:366
  156.0 6.0 %apply.3.refs_0_ = f32[64,8,128]{2,1,0:T(8,128)S(1)} custom-call(bf16[64,64,128]{2,1,0:T(8,128)(2,1)S(1)} %copy-done.1, bf16[128,48,128]{2,1,0:T(8,128)(2,1)S(1)} %get-tuple-element.25.received, s32[128]{0:T(128)S(1)} %multiply_add_fusion.where, s32[384]{0:T(512)S(1)} %convert_element_type.20.asked.refs_6_), custom_call_target="tpu_custom_call" | custom-call | tf_op jit(solution)/shard_map/apply/pallas_call | solution.py:366
  161.9 21.6 %finish.1 = (f32[8,4096]{1,0:T(8,128)S(1)}, f32[16,128]{1,0:T(8,128)S(1)}, f32[16,128]{1,0:T(8,128)S(1)}) custom-call(f32[64,8,128]{2,1,0:T(8,128)S(1)} %apply.3.refs_0_, f32[64,128]{1,0:T(8,128)S(1)} %get-tuple-element.22.refs_1_, f32[16,4096]{1,0:T(8,128)S(1)} %get-tuple-element.26.refs_2_, f32[16,4096]{1,0:T(8,128)S(1)} %get-tuple-element.23.refs_2_.refs_3_, ...), custom_call_target="tpu_custom_call" | custom-call | tf_op jit(solution)/shard_map/finish/pallas_call | solution.py:366
  183.5 0.7 pad_maximum_fusion
  184.3 0.6 pad_maximum_fusion.1
  (10 shorter events, 0.1 us)
Async XLA Ops:
  0.6 1.0 copy-start
  1.6 2.5 %copy-start.1 = (bf16[64,64,128]{2,1,0:T(8,128)(2,1)S(1)}, bf16[64,64,128]{2,1,0:T(8,128)(2,1)}, u32[]{:S(2)}) copy-start(bf16[64,64,128]{2,1,0:T(8,128)(2,1)} %tiles.7) | copy-start | bytes 3145732
  1.6 2.5 %copy-start.2 = (f32[8,4096]{1,0:T(8,128)S(1)}, f32[8,4096]{1,0:T(8,128)}, u32[]{:S(2)}) copy-start(f32[8,4096]{1,0:T(8,128)} %start.1) | copy-start | bytes 393220

commit v3 on v0

v3 whole, which is shorter than its diff:
```python
import functools
import math

import jax
import jax.numpy as jnp
from jax import lax
from jax.experimental import pallas as pl
from jax.experimental.pallas import tpu as pltpu
from jax.sharding import PartitionSpec as P

CAP = 3
MESH = pl.DeviceIdType.MESH
VMEM = pl.BlockSpec(memory_space=pltpu.VMEM)
SMEM = pl.BlockSpec(memory_space=pltpu.SMEM)
F32 = jnp.float32
BF16 = jnp.bfloat16
LIMIT = 32 << 20
EXACT = lax.Precision.HIGHEST


def dot(left, right):
    return jnp.dot(left, right, precision=EXACT, preferred_element_type=F32)


def dot_t(left, right):
    dims = (((1,), (1,)), ((), ()))
    return lax.dot_general(left, right, dims, precision=EXACT, preferred_element_type=F32)


def swap(x):
    return pltpu.roll(x, 64, 1)


def is_low(shape):
    return lax.broadcasted_iota(jnp.int32, shape, 1) < 64


def pair_up(first, second):
    low = is_low(first.shape)
    return jnp.where(low, first, swap(second)), jnp.where(low, swap(first), second)


class Place:
    def __init__(self, sizes):
        self.nx, self.nz, self.ny = sizes
        self.groups = self.nx * self.nz * self.ny
        self.me, self.sub = lax.axis_index("rows"), lax.axis_index("sub")
        self.x = self.me // (self.nz * self.ny)
        self.z = lax.rem(self.me // self.ny, self.nz)
        self.y = lax.rem(self.me, self.ny)
        self.other = (self.me, 1 - self.sub)
        nx, nz, ny = sizes
        self.plane = [self.at(a, 0, b, 0) for a in range(nx) for b in range(ny)][1:]
        self.line = [self.at(0, a, 0, s) for a in range(nz) for s in range(2)][1:]
        self.slots = (self.x * ny + self.y, self.z * 2 + self.sub)

    def at(self, dx, dz, dy, ds):
        x, z, y = lax.rem(self.x + dx, self.nx), lax.rem(self.z + dz, self.nz), lax.rem(self.y + dy, self.ny)
        return ((x * self.nz + z) * self.ny + y, lax.rem(self.sub + ds, 2))

    def peer(self, i):
        return (lax.rem(self.me + i, self.groups), self.sub)


def signal(barrier, device):
    pl.semaphore_signal(barrier, inc=1, device_id=device, device_id_type=MESH)


def meet(place, everyone):
    barrier = pltpu.get_barrier_semaphore()
    if everyone:
        def greet(i, carry):
            signal(barrier, place.peer(i))
            return carry

        lax.fori_loop(1, place.groups, greet, 0, unroll=8)
        rest = [d for k, d in enumerate(place.line) if k % 2 == 0]
        count = place.groups - 1 + len(rest)
    else:
        rest = place.plane + place.line
        count = len(rest)
    for device in rest:
        signal(barrier, device)
    return lambda: pl.semaphore_wait(barrier, count)


def remote(src, dst, send_sem, recv_sem, device):
    return pltpu.make_async_remote_copy(
        src_ref=src, dst_ref=dst, send_sem=send_sem, recv_sem=recv_sem, device_id=device, device_id_type=MESH
    )


class Total:
    def __init__(self, place, near, far, send_sem, recv_sem):
        self.hops = ((near, place.slots[0], place.plane), (far, place.slots[1], place.line))
        self.sems = (send_sem, recv_sem)

    def copy(self, k, ref, device):
        return remote(ref, ref, self.sems[0].at[k], self.sems[1].at[k], device)

    def start(self, k, value):
        held, slot, peers = self.hops[k]
        held[pl.ds(slot, 1)] = value[None]
        for device in peers:
            self.copy(k, held.at[slot], device).start()

    def finish(self, k):
        held, _, peers = self.hops[k]
        self.copy(k, held.at[pl.ds(0, len(peers))], peers[0]).wait()
        return jnp.sum(held[...], axis=0)


class Exchange:
    def __init__(self, place, src, dst, send_sem, recv_sem, own_sem, rows=None):
        self.place, self.src, self.dst = place, src, dst
        self.sems, self.own_sem, self.rows = (send_sem, recv_sem), own_sem, rows

    def part(self, ref, i):
        return ref.at[i] if self.rows is None else ref.at[i, self.rows]

    def own(self):
        me = self.place.me
        return pltpu.make_async_copy(self.part(self.src, me), self.part(self.dst, me), self.own_sem)

    def start(self, build, unroll=2):
        place = self.place
        build(place.me)
        self.own().start()

        def send(i, carry):
            device = place.peer(i)
            build(device[0])
            remote(self.part(self.src, device[0]), self.part(self.dst, place.me), *self.sems, device).start()
            return carry

        lax.fori_loop(1, place.groups, send, 0, unroll=unroll)

    def rest(self):
        rest = pl.ds(0, self.place.groups - 1)
        return remote(self.part(self.src, rest), self.part(self.dst, rest), *self.sems, self.place.peer(1))

    def receive(self):
        self.own().wait()
        self.rest().wait_recv()

    def sent(self):
        self.rest().wait_send()

def factor(gram):
    n = gram.shape[0]
    row = lax.broadcasted_iota(jnp.int32, (n, n), 0)
    col = lax.broadcasted_iota(jnp.int32, (n, n), 1)
    left = gram
    right = jnp.where(row == col, 1.0, 0.0).astype(F32)
    below = lax.broadcasted_iota(jnp.int32, (n, 1), 0)
    for i in range(n):
        share = jnp.where(below > i, left[:, i : i + 1] / left[i : i + 1, i : i + 1], 0.0)
        right = right - share * right[i : i + 1, :]
        left = left - share * left[i : i + 1, :]
    pivots = jnp.sum(jnp.where(row == col, left, 0.0), axis=1, keepdims=True)
    root = lax.rsqrt(pivots)
    return jnp.where(col >= row, left * root, 0.0), right * root


def widen(x):
    return jnp.concatenate([x, jnp.zeros((x.shape[0], 128 - x.shape[1]), F32)], axis=1)


def kernel(
    sizes, blocks, nodes, tiles, start, names, out_ids, placed, where, bases, coeffs,
    full, first_stack, second_stack, named, out_columns, in_columns, own_degree, degree, their_degree, scale,
    in_ids, ids, onehot, scaled, mirrored, chunks, received, partners, returned, product, theirs,
    near, far, tsend, trecv, csend, crecv, cown, xsend, xrecv, asend, arecv, aown, isend, irecv, iown, id_sem,
):
    place = Place(sizes)
    ready = meet(place, True)
    groups, sub = place.groups, place.sub
    columns = full.shape[1]
    half = columns // 2
    own_half = pl.ds(pl.multiple_of(sub * half, 128), half)
    own_rows = pl.ds(pl.multiple_of(sub * 8, 8), 8)
    totals = [Total(place, near.at[i], far.at[i], tsend.at[i], trecv.at[i]) for i in range(3)]

    def pair(i, src, dst):
        return remote(src, dst, xsend.at[i], xrecv.at[i], place.other)

    full[own_rows, :] = start[...]
    named[2 * blocks] = jnp.broadcast_to(names[pl.ds(2 * blocks, 1), :], (8, 128))
    scaled[blocks] = jnp.zeros((8, 128), F32)
    mirrored[2 * blocks] = jnp.zeros((8, 128), F32)
    across = (((1,), (1,)), ((), ()))

    def sums(b, carry):
        tile = tiles[b]
        down = jnp.dot(jnp.ones((8, 64), BF16), tile, preferred_element_type=F32)
        low = is_low(down.shape)
        named[2 * b] = jnp.where(low, down, names[pl.ds(2 * b, 1), :])
        named[2 * b + 1] = jnp.where(low, swap(down), names[pl.ds(2 * b + 1, 1), :])
        along = lax.dot_general(jnp.ones((8, 128), BF16), tile, across, preferred_element_type=F32)
        own_degree[pl.ds(b, 1), :] = jnp.concatenate([along, along], axis=1)[0:1]
        return carry

    lax.fori_loop(0, blocks, sums, 0, unroll=4)

    def fill(d, carry):
        for k in range(CAP):
            out_columns[d, pl.ds(k, 1), :] = named[placed[CAP * d + k]][0:1]
        return carry

    lax.fori_loop(0, groups, fill, 0, unroll=4)
    ready()
    swap_rows = pair(0, start, full.at[own_rows])
    swap_rows.start()
    sent_columns = Exchange(place, out_columns, in_columns, csend, crecv, cown)
    sent_columns.start(lambda d: None, unroll=4)
    swap_rows.wait()
    part = full[:, own_half]
    totals[0].start(0, widen(dot_t(part, part)))

    sent_ids = Exchange(place, out_ids, in_ids, isend, irecv, iown)
    sent_ids.start(lambda d: None, unroll=4)

    sent_columns.receive()
    sums_in = jnp.zeros((blocks, 128), F32)
    for k in range(CAP):
        rows = in_columns[:, k, :]
        index = lax.broadcasted_iota(jnp.int32, (blocks, groups), 0).astype(F32)
        match = jnp.where(index == rows.T[64:65, :], 1.0, 0.0).astype(F32)
        onehot[k] = match.astype(BF16)
        sums_in = sums_in + dot(match, rows)
    degree[...] = own_degree[...] + jnp.where(is_low(sums_in.shape), sums_in, swap(sums_in))
    swap_degree = pair(1, degree, their_degree)
    swap_degree.start()
    totals[0].start(1, totals[0].finish(0))
    sent_columns.sent()
    sent_ids.receive()
    id_copy = pltpu.make_async_copy(in_ids, ids, id_sem)
    id_copy.start()
    sent_ids.sent()
    id_copy.wait()
    swap_degree.wait()
    scale[...] = lax.rsqrt(degree[...] + their_degree[...])
    _, inverse = factor(totals[0].finish(1)[:, :16])
    first_stack[16:32] = dot(inverse, full[...])

    def scale_of(b):
        return jnp.broadcast_to(scale[pl.ds(b, 1), :], (8, 128))

    def block_rows(b):
        return pl.ds(pl.multiple_of(b * 8, 8), 8)

    for m, stack in enumerate((first_stack, second_stack)):
        def scale_blocks(t, carry):
            lanes = pl.ds(pl.multiple_of(t * 128, 128), 128)
            pairs = pair_up(stack[16:24, lanes], stack[24:32, lanes])
            for p in range(2):
                scaled[2 * t + p] = pairs[p] * scale_of(2 * t + p)
            return carry

        lax.fori_loop(0, blocks // 2, scale_blocks, 0, unroll=4)

        def mirror(b, carry):
            block = scaled[b]
            left = jnp.concatenate([block, swap(block)], axis=0)[:, :64].astype(BF16)
            out = jnp.dot(left, tiles[b], preferred_element_type=F32)
            mirrored[2 * b], mirrored[2 * b + 1] = pair_up(out[0:8], out[8:16])
            return carry

        def builder(k):
            def build(d):
                parts = []
                for slot in (2 * k, 2 * k + 1):
                    if slot < CAP:
                        parts.append(scaled[jnp.clip(ids[d, 0, slot], 0, blocks)])
                    else:
                        parts.append(mirrored[placed[CAP * d + slot - CAP]])
                chunks[d, pl.ds(16 * k, 16), :] = jnp.concatenate(parts, axis=0).astype(BF16)

            return build

        parts = [
            Exchange(
                place, chunks, received.at[m], asend.at[m, k], arecv.at[m, k], aown.at[m, k], pl.ds(16 * k, 16)
            )
            for k in range(CAP)
        ]
        parts[0].start(builder(0))
        lax.fori_loop(0, blocks, mirror, 0, unroll=4)
        parts[1].start(builder(1))
        parts[2].start(builder(2))
        rest = stack[16:, own_half]
        rest = dot_t(rest, rest)

        parts[0].receive()
        parts[1].receive()

        def spread(d, carry):
            chunk = received[m, d, pl.ds(0, 32), :].astype(F32)
            for k in range(CAP):
                partners[d * CAP + k] = chunk[8 * k : 8 * k + 8]
            returned[pl.ds(pl.multiple_of(d * 24, 8), 8), :] = chunk[24:32]
            return carry

        lax.fori_loop(0, groups, spread, 0, unroll=4)

        def forward(b, carry):
            low, high = pair_up(partners[where[2 * b]], partners[where[2 * b + 1]])
            left = jnp.concatenate([low, high], axis=0).astype(BF16)
            out = lax.dot_general(left, tiles[b], across, preferred_element_type=F32)
            product[block_rows(b), :] = jnp.concatenate([out[0:8], out[8:16]], axis=1)
            return carry

        lax.fori_loop(0, blocks, forward, 0, unroll=4)
        parts[2].receive()

        def spread_last(d, carry):
            chunk = received[m, d, pl.ds(32, 16), :].astype(F32)
            returned[pl.ds(pl.multiple_of(d * 24 + 8, 8), 16), :] = chunk
            return carry

        lax.fori_loop(0, groups, spread_last, 0, unroll=4)
        for j in range(8):
            added = jnp.zeros((blocks, 128), F32)
            for k in range(CAP):
                rows = returned[pl.ds(8 * k + j, groups, stride=24), :].astype(BF16)
                added = added + jnp.dot(onehot[k], rows, preferred_element_type=F32)
            lines = pl.ds(j, blocks, stride=8)
            product[lines, :] = product[lines, :] + added

        height = blocks * 4
        halves = [pl.ds(pl.multiple_of(s * height, 8), height) for s in (1 - sub, sub)]
        swaps = [pair(2 + 2 * m + i, product.at[h], theirs.at[m, h]) for i, h in enumerate(halves)]
        for one in swaps:
            one.start()
        for part in parts:
            part.sent()

        def residual(first):
            def step(t, carry):
                t = first + t
                lanes = pl.ds(pl.multiple_of(t * 128, 128), 128)
                both = []
                for p in range(2):
                    b = 2 * t + p
                    both.append((product[block_rows(b), :] + theirs[m, block_rows(b), :]) * scale_of(b))
                stack[0:8, lanes], stack[8:16, lanes] = pair_up(both[0], both[1])
                return carry

            lax.fori_loop(0, blocks // 4, step, 0, unroll=4)

        swaps[0].wait()
        residual(sub * (blocks // 4))
        cross = dot_t(stack[0:16, own_half], stack[:, own_half])
        packed = [cross, rest[0:16]] + ([rest[16:32, 16:32]] if m else [])
        totals[m + 1].start(0, widen(jnp.concatenate(packed, axis=1)))
        swaps[1].wait()
        residual((1 - sub) * (blocks // 4))
        totals[m + 1].start(1, totals[m + 1].finish(0))
        packed = totals[m + 1].finish(1)
        cut = [packed[:, 16 * k : 16 * k + 16] for k in range(6)]
        row = lax.broadcasted_iota(jnp.int32, (16, 16), 0)
        col = lax.broadcasted_iota(jnp.int32, (16, 16), 1)
        eye = jnp.where(row == col, 1.0, 0.0).astype(F32)
        if m:
            rr, rq, rp, qq, qp, pp = cut
            lines = [[rr, rq, rp], [rq.T, qq, qp], [rp.T, qp.T, pp]]
        else:
            rr, rq, qq = cut[:3]
            lines = [[rr, rq], [rq.T, qq]]
        gram = jnp.concatenate([jnp.concatenate(line, axis=1) for line in lines], axis=0)
        alpha = qq - rq.T
        mix = [-eye, eye - alpha.T] + ([-coeffs[1]] if m else [])
        mix = jnp.concatenate(mix, axis=1)
        upper, inverse = factor(dot_t(dot(mix, gram), mix))
        coeffs[2 * m] = alpha
        coeffs[2 * m + 1] = upper
        following = dot(dot(inverse, mix), stack[...])
        if m:
            full[...] = following
            bases[1] = full[own_rows, :] * math.sqrt(nodes)
        else:
            second_stack[16:32] = following
            second_stack[32:48] = first_stack[16:32]
            bases[0] = second_stack[pl.ds(pl.multiple_of(16 + sub * 8, 8), 8), :] * math.sqrt(nodes)


def local(sizes, upper_tiles, tile_clusters, cluster_slot, start_block):
    nx, nz, ny = sizes
    blocks, cluster, _ = upper_tiles.shape
    groups = nx * nz * ny
    columns = blocks * cluster
    count = 2 * blocks
    targets = cluster_slot.at[tile_clusters].get(mode="promise_in_bounds").reshape(-1)
    owners = targets // blocks
    order = jnp.arange(count, dtype=jnp.int32)
    before = (owners[:, None] == owners[None, :]) & (order[None, :] < order[:, None])
    where = owners * CAP + jnp.sum(before.astype(jnp.int32), axis=1)
    taken = where[None, :] == jnp.arange(groups * CAP, dtype=jnp.int32)[:, None]
    placed = count - jnp.sum(jnp.where(taken, count - order[None, :], 0), axis=1)
    inside = targets % blocks
    out_ids = blocks - jnp.sum(jnp.where(taken, blocks - inside[None, :], 0), axis=1)
    out_ids = jnp.pad(out_ids.reshape(groups, 1, CAP), ((0, 0), (0, 0), (0, 128 - CAP)))
    names = jnp.concatenate([inside, jnp.full((1,), blocks, jnp.int32)])
    names = jnp.broadcast_to(names.astype(F32)[:, None], (count + 1, 128))

    dma = pltpu.SemaphoreType.DMA
    block = lambda n: pltpu.VMEM((n, 8, 128), F32)
    wide = lambda *shape: pltpu.VMEM(shape + (128,), F32)
    scratch = [
        pltpu.VMEM((16, columns), F32),
        pltpu.VMEM((32, columns), F32),
        pltpu.VMEM((48, columns), F32),
        block(count + 1),
        wide(groups, CAP),
        wide(groups, CAP),
        wide(blocks),
        wide(blocks),
        wide(blocks),
        wide(blocks),
        pltpu.VMEM((groups, 1, 128), jnp.int32),
        pltpu.SMEM((groups, 1, 128), jnp.int32),
        pltpu.VMEM((CAP, blocks, groups), BF16),
        block(blocks + 1),
        block(count + 1),
        pltpu.VMEM((groups, 16 * CAP, 128), BF16),
        pltpu.VMEM((2, groups, 16 * CAP, 128), BF16),
        block(groups * CAP),
        wide(groups * CAP * 8 + CAP * 8),
        wide(blocks * 8 + 8),
        wide(2, blocks * 8),
        wide(3, nx * ny, 16),
        wide(3, nz * 2, 16),
        dma((3, 2)),
        dma((3, 2)),
        dma,
        dma,
        dma,
        dma((6,)),
        dma((6,)),
        dma((2, CAP)),
        dma((2, CAP)),
        dma((2, CAP)),
        dma,
        dma,
        dma,
        dma,
    ]
    return pl.pallas_call(
        functools.partial(kernel, sizes, blocks, columns * groups),
        out_shape=[
            jax.ShapeDtypeStruct((2, 8, columns), F32),
            jax.ShapeDtypeStruct((4, 16, 16), F32),
        ],
        in_specs=[VMEM, VMEM, VMEM, VMEM, SMEM, SMEM],
        out_specs=[VMEM, VMEM],
        scratch_shapes=scratch,
        compiler_params=pltpu.CompilerParams(collective_id=1, has_side_effects=True, vmem_limit_bytes=LIMIT),
        name="lanczos",
    )(upper_tiles, start_block, names, out_ids, placed, where)


def solution(mesh):
    sizes = (4, 8, 4)
    in_specs = (P("rows", None, "sub"), P("rows", "sub"), P(), P("sub", "rows"))
    out_specs = (P(None, "sub", "rows"), P())
    body = functools.partial(local, sizes)
    return jax.shard_map(body, mesh=mesh, in_specs=in_specs, out_specs=out_specs, check_vma=False)
```

time: 2160 us -> 152 us (0.07)
  blocking collectives: 1760 us -> 0 us
  Pallas kernels: 0 us -> 145 us
  waiting for transfers between devices: 132 us -> 0 us
  local copies, waits for them, and re-layouts: 90.2 us -> 4.26 us
  other arithmetic: 81.1 us -> 0.4 us
  starting transfers between devices: 63.8 us -> 0 us
    psum x6 -> x0, blocking collectives: 1760 us -> none  [the longest x2 709 us: local(): gram = lax.psum(inner(residual, residual), 'rows')]
    pallas_call x0 -> x1, Pallas kernels: none -> 145 us  [local(): pl.pallas_call(functools.partial(kernel, sizes, blocks, columns * groups)...]
    all_to_all x6 -> x0, waiting for transfers between devices: 82.3 us -> none  [the longest x2 65.7 us: local(): lax.all_to_all(outgoing.reshape(groups, capacity, width_k * cluster), 'ro...]
    scatter-add x3 -> x0, other arithmetic: 64.8 us -> none  [the longest x2 62.2 us: local(): summed = forward.at[asked].add(returned)]
    all_to_all x6 -> x0, starting transfers between devices: 63.7 us -> none  [the longest x2 22.5 us: local(): lax.all_to_all(outgoing.reshape(groups, capacity, width_k * cluster), 'ro...]
    psum x2 -> x0, waiting for transfers between devices: 50.1 us -> none  [local(): product = lax.psum(product, 'sub')]
    reshape x18 -> x0, local copies, waits for them, and re-layouts: 38 us -> none  [the longest x2 9.06 us: local(): returned = returned.reshape(groups * capacity, width_k, cluster)]
    scatter x4 -> x0, local copies, waits for them, and re-layouts: 32.7 us -> none  [the longest x2 30.8 us: local(): jnp.zeros((groups * capacity, width_k, cluster), jnp.float32).at[slots]]
  transfers between devices with their start and end apart: 8 -> 0, of which waited for: 6 -> 0; matrix products, arithmetic and copies ran while one was open for 3% -> 0% of each run, Pallas kernels for 0% -> 0%
where the time goes in v3:
time: 152 us; the launch traced here: 150 us
  Pallas kernels  145 us (95%)
  local copies, waits for them, and re-layouts  4.26 us (3%)
    pallas_call x1, Pallas kernels, local(): pl.pallas_call(functools.partial(kernel, sizes, blocks, columns * groups)...  145 us

profile of v3, /device:TPU:8, one launch (start us, length us, event | category | flops | bytes accessed | tf_op | source)
XLA Modules:
  0.0 150.1 jit_solution(15735761083310883200)
XLA Ops:
  0.6 0.0 copy-start
  0.6 0.0 copy-start.3
  0.7 0.7 copy-done.3
  1.3 0.1 copy.9
  1.4 0.1 reshape.134
  1.6 0.0 copy-done
  1.6 0.0 copy-start.1
  1.6 1.1 gather_fusion
  2.8 0.2 convert_reduce_fusion
  3.0 0.2 select_reduce_fusion
  3.2 0.0 copy-start.2
  3.2 0.2 sub.52
  3.5 0.1 broadcast_in_dim.36.names
  3.5 0.0 copy-done.1
  3.5 0.5 copy-done.2
  4.1 144.7 %lanczos.1 = (f32[2,8,4096]{2,1,0:T(8,128)S(1)}, f32[4,16,16]{2,1,0:T(8,128)S(1)}) custom-call(bf16[64,64,128]{2,1,0:T(8,128)(2,1)S(1)} %copy-done.1, f32[8,4096]{1,0:T(8,128)S(1)} %copy-done.2, f32[129,128]{1,0:T(8,128)S(1)} %broadcast_in_dim.36.names, s32[128,1,128]{2,1,0:T(1,128)S(1)} %pad.4.out_ids, s32[384]{0:T(512)S(1)} %get-tuple-element.7.placed, ...), custom_call_target="tpu_custom_call" | custom-call | tf_op jit(solution)/shard_map/lanczos/pallas_call | solution.py:448
  148.8 0.7 copy.13
  149.5 0.6 copy.14
  (8 shorter events, 0.1 us)
Async XLA Ops:
  0.6 1.0 copy-start
  0.6 0.7 copy-start.3
  1.6 1.9 %copy-start.1 = (bf16[64,64,128]{2,1,0:T(8,128)(2,1)S(1)}, bf16[64,64,128]{2,1,0:T(8,128)(2,1)}, u32[]{:S(2)}) copy-start(bf16[64,64,128]{2,1,0:T(8,128)(2,1)} %tiles.1) | copy-start | bytes 3145732
  3.2 0.9 copy-start.2

commit v4 on v3

--- a/solution.py
+++ b/solution.py
@@ -162,15 +162,35 @@
     return jnp.where(col >= row, left * root, 0.0), right * root
 
 
-def widen(x):
-    return jnp.concatenate([x, jnp.zeros((x.shape[0], 128 - x.shape[1]), F32)], axis=1)
+def fold(x):
+    width = x.shape[1]
+    return jnp.concatenate([x[0:8], x[8:16], jnp.zeros((8, 128 - 2 * width), F32)], axis=1)
+
+
+def unfold(x, width):
+    return jnp.concatenate([x[:, :width], x[:, width : 2 * width]], axis=0)
+
+
+def pieces(x):
+    high = x.astype(BF16)
+    rest = x - high.astype(F32)
+    middle = rest.astype(BF16)
+    return jnp.concatenate([high, middle, (rest - middle.astype(F32)).astype(BF16)], axis=0)
+
+
+def gram_of(left, right):
+    rows, width = left.shape[0], right.shape[0]
+    dims = (((1,), (1,)), ((), ()))
+    out = lax.dot_general(pieces(left), pieces(right), dims, preferred_element_type=F32)
+    out = out[0:rows] + out[rows : 2 * rows] + out[2 * rows :]
+    return out[:, :width] + out[:, width : 2 * width] + out[:, 2 * width :]
 
 
 def kernel(
-    sizes, blocks, nodes, tiles, start, names, out_ids, placed, where, bases, coeffs,
+    sizes, blocks, nodes, tiles, start, names, placed, where, bases, coeffs,
     full, first_stack, second_stack, named, out_columns, in_columns, own_degree, degree, their_degree, scale,
-    in_ids, ids, onehot, scaled, mirrored, chunks, received, partners, returned, product, theirs,
-    near, far, tsend, trecv, csend, crecv, cown, xsend, xrecv, asend, arecv, aown, isend, irecv, iown, id_sem,
+    onehot, onehot_t, scaled, mirrored, reply, chunks, received, partners, returned, product, theirs,
+    near, far, tsend, trecv, csend, crecv, cown, xsend, xrecv, asend, arecv, aown,
 ):
     place = Place(sizes)
     ready = meet(place, True)
@@ -179,14 +199,13 @@
     half = columns // 2
     own_half = pl.ds(pl.multiple_of(sub * half, 128), half)
     own_rows = pl.ds(pl.multiple_of(sub * 8, 8), 8)
-    totals = [Total(place, near.at[i], far.at[i], tsend.at[i], trecv.at[i]) for i in range(3)]
+    totals = [Total(place, near.at[i], far.at[i], tsend.at[i], trecv.at[i]) for i in range(5)]
 
     def pair(i, src, dst):
         return remote(src, dst, xsend.at[i], xrecv.at[i], place.other)
 
     full[own_rows, :] = start[...]
     named[2 * blocks] = jnp.broadcast_to(names[pl.ds(2 * blocks, 1), :], (8, 128))
-    scaled[blocks] = jnp.zeros((8, 128), F32)
     mirrored[2 * blocks] = jnp.zeros((8, 128), F32)
     across = (((1,), (1,)), ((), ()))
 
@@ -202,23 +221,21 @@
 
     lax.fori_loop(0, blocks, sums, 0, unroll=4)
 
+    ready()
+    swap_rows = pair(0, start, full.at[own_rows])
+    swap_rows.start()
+
     def fill(d, carry):
         for k in range(CAP):
             out_columns[d, pl.ds(k, 1), :] = named[placed[CAP * d + k]][0:1]
         return carry
 
     lax.fori_loop(0, groups, fill, 0, unroll=4)
-    ready()
-    swap_rows = pair(0, start, full.at[own_rows])
-    swap_rows.start()
+    swap_rows.wait()
+    totals[0].start(0, fold(gram_of(full[:, own_half], full[:, own_half])))
     sent_columns = Exchange(place, out_columns, in_columns, csend, crecv, cown)
     sent_columns.start(lambda d: None, unroll=4)
-    swap_rows.wait()
-    part = full[:, own_half]
-    totals[0].start(0, widen(dot_t(part, part)))
-
-    sent_ids = Exchange(place, out_ids, in_ids, isend, irecv, iown)
-    sent_ids.start(lambda d: None, unroll=4)
+    totals[0].start(1, totals[0].finish(0))
 
     sent_columns.receive()
     sums_in = jnp.zeros((blocks, 128), F32)
@@ -226,21 +243,17 @@
         rows = in_columns[:, k, :]
         index = lax.broadcasted_iota(jnp.int32, (blocks, groups), 0).astype(F32)
         match = jnp.where(index == rows.T[64:65, :], 1.0, 0.0).astype(F32)
+        index = lax.broadcasted_iota(jnp.int32, (groups, blocks), 1).astype(F32)
+        onehot_t[k] = jnp.where(index == rows[:, 64:65], 1.0, 0.0).astype(BF16)
         onehot[k] = match.astype(BF16)
         sums_in = sums_in + dot(match, rows)
     degree[...] = own_degree[...] + jnp.where(is_low(sums_in.shape), sums_in, swap(sums_in))
     swap_degree = pair(1, degree, their_degree)
     swap_degree.start()
-    totals[0].start(1, totals[0].finish(0))
     sent_columns.sent()
-    sent_ids.receive()
-    id_copy = pltpu.make_async_copy(in_ids, ids, id_sem)
-    id_copy.start()
-    sent_ids.sent()
-    id_copy.wait()
     swap_degree.wait()
     scale[...] = lax.rsqrt(degree[...] + their_degree[...])
-    _, inverse = factor(totals[0].finish(1)[:, :16])
+    _, inverse = factor(unfold(totals[0].finish(1), 16))
     first_stack[16:32] = dot(inverse, full[...])
 
     def scale_of(b):
@@ -254,27 +267,35 @@
             lanes = pl.ds(pl.multiple_of(t * 128, 128), 128)
             pairs = pair_up(stack[16:24, lanes], stack[24:32, lanes])
             for p in range(2):
-                scaled[2 * t + p] = pairs[p] * scale_of(2 * t + p)
+                scaled[block_rows(2 * t + p), :] = pairs[p] * scale_of(2 * t + p)
             return carry
 
         lax.fori_loop(0, blocks // 2, scale_blocks, 0, unroll=4)
 
         def mirror(b, carry):
-            block = scaled[b]
+            block = scaled[block_rows(b), :]
             left = jnp.concatenate([block, swap(block)], axis=0)[:, :64].astype(BF16)
             out = jnp.dot(left, tiles[b], preferred_element_type=F32)
             mirrored[2 * b], mirrored[2 * b + 1] = pair_up(out[0:8], out[8:16])
             return carry
 
+        def answer(slots):
+            for j in range(8):
+                rows = scaled[pl.ds(j, blocks, stride=8), :].astype(BF16)
+                for k in slots:
+                    chosen = jnp.dot(onehot_t[k], rows, preferred_element_type=F32)
+                    reply[pl.ds(8 * k + j, groups, stride=24), :] = chosen
+
         def builder(k):
             def build(d):
-                parts = []
-                for slot in (2 * k, 2 * k + 1):
-                    if slot < CAP:
-                        parts.append(scaled[jnp.clip(ids[d, 0, slot], 0, blocks)])
-                    else:
-                        parts.append(mirrored[placed[CAP * d + slot - CAP]])
-                chunks[d, pl.ds(16 * k, 16), :] = jnp.concatenate(parts, axis=0).astype(BF16)
+                if k == 0:
+                    value = reply[pl.ds(pl.multiple_of(24 * d, 8), 16), :]
+                elif k == 1:
+                    last = reply[pl.ds(pl.multiple_of(24 * d + 16, 8), 8), :]
+                    value = jnp.concatenate([last, mirrored[placed[CAP * d]]], axis=0)
+                else:
+                    value = jnp.concatenate([mirrored[placed[CAP * d + s]] for s in (1, 2)], axis=0)
+                chunks[d, pl.ds(16 * k, 16), :] = value.astype(BF16)
 
             return build
 
@@ -284,12 +305,16 @@
             )
             for k in range(CAP)
         ]
-        parts[0].start(builder(0))
+        answer((0, 1))
+        parts[0].start(builder(0), unroll=4)
+        answer((2,))
         lax.fori_loop(0, blocks, mirror, 0, unroll=4)
         parts[1].start(builder(1))
         parts[2].start(builder(2))
-        rest = stack[16:, own_half]
-        rest = dot_t(rest, rest)
+        known = gram_of(stack[16:, own_half], stack[16:, own_half])
+        if m:
+            known = jnp.concatenate([known[0:16], known[16:32, 16:32]], axis=1)
+        totals[3 + m].start(0, fold(known))
 
         parts[0].receive()
         parts[1].receive()
@@ -332,6 +357,7 @@
         swaps = [pair(2 + 2 * m + i, product.at[h], theirs.at[m, h]) for i, h in enumerate(halves)]
         for one in swaps:
             one.start()
+        totals[m + 3].start(1, totals[m + 3].finish(0))
         for part in parts:
             part.sent()
 
@@ -350,14 +376,13 @@
 
         swaps[0].wait()
         residual(sub * (blocks // 4))
-        cross = dot_t(stack[0:16, own_half], stack[:, own_half])
-        packed = [cross, rest[0:16]] + ([rest[16:32, 16:32]] if m else [])
-        totals[m + 1].start(0, widen(jnp.concatenate(packed, axis=1)))
+        totals[m + 1].start(0, fold(gram_of(stack[0:16, own_half], stack[:, own_half])))
         swaps[1].wait()
         residual((1 - sub) * (blocks // 4))
         totals[m + 1].start(1, totals[m + 1].finish(0))
-        packed = totals[m + 1].finish(1)
-        cut = [packed[:, 16 * k : 16 * k + 16] for k in range(6)]
+        known = unfold(totals[m + 3].finish(1), 48 if m else 16)
+        cross = unfold(totals[m + 1].finish(1), 48 if m else 32)
+        cut = [x[:, 16 * k : 16 * k + 16] for x in (cross, known) for k in range(x.shape[1] // 16)]
         row = lax.broadcasted_iota(jnp.int32, (16, 16), 0)
         col = lax.broadcasted_iota(jnp.int32, (16, 16), 1)
         eye = jnp.where(row == col, 1.0, 0.0).astype(F32)
@@ -365,7 +390,7 @@
             rr, rq, rp, qq, qp, pp = cut
             lines = [[rr, rq, rp], [rq.T, qq, qp], [rp.T, qp.T, pp]]
         else:
-            rr, rq, qq = cut[:3]
+            rr, rq, qq = cut
             lines = [[rr, rq], [rq.T, qq]]
         gram = jnp.concatenate([jnp.concatenate(line, axis=1) for line in lines], axis=0)
         alpha = qq - rq.T
@@ -398,8 +423,6 @@
     taken = where[None, :] == jnp.arange(groups * CAP, dtype=jnp.int32)[:, None]
     placed = count - jnp.sum(jnp.where(taken, count - order[None, :], 0), axis=1)
     inside = targets % blocks
-    out_ids = blocks - jnp.sum(jnp.where(taken, blocks - inside[None, :], 0), axis=1)
-    out_ids = jnp.pad(out_ids.reshape(groups, 1, CAP), ((0, 0), (0, 0), (0, 128 - CAP)))
     names = jnp.concatenate([inside, jnp.full((1,), blocks, jnp.int32)])
     names = jnp.broadcast_to(names.astype(F32)[:, None], (count + 1, 128))
 
@@ -417,21 +440,21 @@
         wide(blocks),
         wide(blocks),
         wide(blocks),
-        pltpu.VMEM((groups, 1, 128), jnp.int32),
-        pltpu.SMEM((groups, 1, 128), jnp.int32),
         pltpu.VMEM((CAP, blocks, groups), BF16),
-        block(blocks + 1),
+        pltpu.VMEM((CAP, groups, blocks), BF16),
+        wide(blocks * 8 + 8),
         block(count + 1),
+        wide(groups * CAP * 8 + CAP * 8),
         pltpu.VMEM((groups, 16 * CAP, 128), BF16),
         pltpu.VMEM((2, groups, 16 * CAP, 128), BF16),
         block(groups * CAP),
         wide(groups * CAP * 8 + CAP * 8),
         wide(blocks * 8 + 8),
         wide(2, blocks * 8),
-        wide(3, nx * ny, 16),
-        wide(3, nz * 2, 16),
-        dma((3, 2)),
-        dma((3, 2)),
+        wide(5, nx * ny, 8),
+        wide(5, nz * 2, 8),
+        dma((5, 2)),
+        dma((5, 2)),
         dma,
         dma,
         dma,
@@ -440,10 +463,6 @@
         dma((2, CAP)),
         dma((2, CAP)),
         dma((2, CAP)),
-        dma,
-        dma,
-        dma,
-        dma,
     ]
     return pl.pallas_call(
         functools.partial(kernel, sizes, blocks, columns * groups),
@@ -451,12 +470,12 @@
             jax.ShapeDtypeStruct((2, 8, columns), F32),
             jax.ShapeDtypeStruct((4, 16, 16), F32),
         ],
-        in_specs=[VMEM, VMEM, VMEM, VMEM, SMEM, SMEM],
+        in_specs=[VMEM, VMEM, VMEM, SMEM, SMEM],
         out_specs=[VMEM, VMEM],
         scratch_shapes=scratch,
         compiler_params=pltpu.CompilerParams(collective_id=1, has_side_effects=True, vmem_limit_bytes=LIMIT),
         name="lanczos",
-    )(upper_tiles, start_block, names, out_ids, placed, where)
+    )(upper_tiles, start_block, names, placed, where)
 
 
 def solution(mesh):

time: 152 us -> 144 us (0.947)
  Pallas kernels: 145 us -> 138 us
    pallas_call x1, Pallas kernels: 145 us -> 138 us  [local(): pl.pallas_call(functools.partial(kernel, sizes, blocks, columns * groups)...]
where the time goes in v4:
time: 144 us; the launch traced here: 142 us
  Pallas kernels  138 us (96%)
  local copies, waits for them, and re-layouts  2.8 us (2%)
    pallas_call x1, Pallas kernels, local(): pl.pallas_call(functools.partial(kernel, sizes, blocks, columns * groups)...  138 us

profile of v4, /device:TPU:8, one launch (start us, length us, event | category | flops | bytes accessed | tf_op | source)
XLA Modules:
  0.0 142.2 jit_solution(17426725284151242745)
XLA Ops:
  0.6 0.0 copy-start
  0.6 0.7 compare_select_fusion
  1.3 0.1 copy.8
  1.4 0.1 reshape.98
  1.6 0.0 copy-done
  1.6 0.0 copy-start.1
  1.6 0.0 copy-start.2
  1.6 1.1 gather_fusion
  2.8 0.2 convert_reduce_fusion
  3.0 0.1 select_reduce_fusion
  3.2 0.1 broadcast_in_dim.17.names
  3.2 0.0 copy-done.1
  3.2 0.0 copy-done.2
  3.3 137.6 %lanczos.1 = (f32[2,8,4096]{2,1,0:T(8,128)S(1)}, f32[4,16,16]{2,1,0:T(8,128)S(1)}) custom-call(bf16[64,64,128]{2,1,0:T(8,128)(2,1)S(1)} %copy-done.1, f32[8,4096]{1,0:T(8,128)S(1)} %copy-done.2, f32[129,128]{1,0:T(8,128)S(1)} %broadcast_in_dim.17.names, s32[384]{0:T(512)S(1)} %broadcast_subtract_fusion.placed, s32[128]{0:T(128)S(1)} %get-tuple-element.5.where), custom_call_target="tpu_custom_call" | custom-call | tf_op jit(solution)/shard_map/lanczos/pallas_call | solution.py:467
  140.9 0.7 copy.11
  141.6 0.6 copy.12
  (5 shorter events, 0.0 us)
Async XLA Ops:
  0.6 1.0 copy-start
  1.6 1.6 %copy-start.1 = (bf16[64,64,128]{2,1,0:T(8,128)(2,1)S(1)}, bf16[64,64,128]{2,1,0:T(8,128)(2,1)}, u32[]{:S(2)}) copy-start(bf16[64,64,128]{2,1,0:T(8,128)(2,1)} %tiles.1) | copy-start | bytes 3145732
  1.6 1.6 %copy-start.2 = (f32[8,4096]{1,0:T(8,128)S(1)}, f32[8,4096]{1,0:T(8,128)}, u32[]{:S(2)}) copy-start(f32[8,4096]{1,0:T(8,128)} %start.1) | copy-start | bytes 393220

commit v5 on v4

--- a/solution.py
+++ b/solution.py
@@ -58,6 +58,16 @@
         x, z, y = lax.rem(self.x + dx, self.nx), lax.rem(self.z + dz, self.nz), lax.rem(self.y + dy, self.ny)
         return ((x * self.nz + z) * self.ny + y, lax.rem(self.sub + ds, 2))
 
+    def order(self):
+        spans = [(0, self.nz // 2)] + [(self.nz // 2 - g, self.nz // 2 + g) for g in range(1, self.nz // 2)]
+        wide = 2 * self.nx * self.ny
+        for g, (one, two) in enumerate(spans):
+            def peer(i, one=one, two=two):
+                dz = one + (two - one) * lax.rem(i, 2)
+                return self.at(i // (2 * self.ny), dz, lax.rem(i // 2, self.ny), 0)
+
+            yield (1 if g == 0 else 0), wide, peer
+
     def peer(self, i):
         return (lax.rem(self.me + i, self.groups), self.sub)
 
@@ -126,14 +136,14 @@
         place = self.place
         build(place.me)
         self.own().start()
-
-        def send(i, carry):
-            device = place.peer(i)
-            build(device[0])
-            remote(self.part(self.src, device[0]), self.part(self.dst, place.me), *self.sems, device).start()
-            return carry
-
-        lax.fori_loop(1, place.groups, send, 0, unroll=unroll)
+        for begin, end, peer in place.order():
+            def send(i, carry):
+                device = peer(i)
+                build(device[0])
+                remote(self.part(self.src, device[0]), self.part(self.dst, place.me), *self.sems, device).start()
+                return carry
+
+            lax.fori_loop(begin, end, send, 0, unroll=unroll)
 
     def rest(self):
         rest = pl.ds(0, self.place.groups - 1)
@@ -187,7 +197,7 @@
 
 
 def kernel(
-    sizes, blocks, nodes, tiles, start, names, placed, where, bases, coeffs,
+    sizes, blocks, nodes, tiles, start, their_start, names, placed, where, bases, coeffs,
     full, first_stack, second_stack, named, out_columns, in_columns, own_degree, degree, their_degree, scale,
     onehot, onehot_t, scaled, mirrored, reply, chunks, received, partners, returned, product, theirs,
     near, far, tsend, trecv, csend, crecv, cown, xsend, xrecv, asend, arecv, aown,
@@ -205,6 +215,7 @@
         return remote(src, dst, xsend.at[i], xrecv.at[i], place.other)
 
     full[own_rows, :] = start[...]
+    full[pl.ds(pl.multiple_of(8 - sub * 8, 8), 8), :] = their_start[...]
     named[2 * blocks] = jnp.broadcast_to(names[pl.ds(2 * blocks, 1), :], (8, 128))
     mirrored[2 * blocks] = jnp.zeros((8, 128), F32)
     across = (((1,), (1,)), ((), ()))
@@ -221,20 +232,16 @@
 
     lax.fori_loop(0, blocks, sums, 0, unroll=4)
 
+    first = fold(gram_of(full[:, own_half], full[:, own_half]))
     ready()
-    swap_rows = pair(0, start, full.at[own_rows])
-    swap_rows.start()
-
-    def fill(d, carry):
+    totals[0].start(0, first)
+
+    def fill(d):
         for k in range(CAP):
             out_columns[d, pl.ds(k, 1), :] = named[placed[CAP * d + k]][0:1]
-        return carry
-
-    lax.fori_loop(0, groups, fill, 0, unroll=4)
-    swap_rows.wait()
-    totals[0].start(0, fold(gram_of(full[:, own_half], full[:, own_half])))
+
     sent_columns = Exchange(place, out_columns, in_columns, csend, crecv, cown)
-    sent_columns.start(lambda d: None, unroll=4)
+    sent_columns.start(fill, unroll=4)
     totals[0].start(1, totals[0].finish(0))
 
     sent_columns.receive()
@@ -415,6 +422,7 @@
     groups = nx * nz * ny
     columns = blocks * cluster
     count = 2 * blocks
+    their_start = lax.ppermute(start_block, "sub", [(0, 1), (1, 0)])
     targets = cluster_slot.at[tile_clusters].get(mode="promise_in_bounds").reshape(-1)
     owners = targets // blocks
     order = jnp.arange(count, dtype=jnp.int32)
@@ -470,12 +478,12 @@
             jax.ShapeDtypeStruct((2, 8, columns), F32),
             jax.ShapeDtypeStruct((4, 16, 16), F32),
         ],
-        in_specs=[VMEM, VMEM, VMEM, SMEM, SMEM],
+        in_specs=[VMEM, VMEM, VMEM, VMEM, SMEM, SMEM],
         out_specs=[VMEM, VMEM],
         scratch_shapes=scratch,
         compiler_params=pltpu.CompilerParams(collective_id=1, has_side_effects=True, vmem_limit_bytes=LIMIT),
         name="lanczos",
-    )(upper_tiles, start_block, names, placed, where)
+    )(upper_tiles, start_block, their_start, names, placed, where)
 
 
 def solution(mesh):

time: 144 us -> 142 us (0.986)
  Pallas kernels: 138 us -> 136 us
    pallas_call x1, Pallas kernels: 138 us -> 136 us  [local(): pl.pallas_call(functools.partial(kernel, sizes, blocks, columns * groups)...]
  transfers between devices with their start and end apart: 0 -> 1, of which waited for: 0 -> 0; matrix products, arithmetic and copies ran while one was open for 0% -> 1% of each run, Pallas kernels for 0% -> 0%
where the time goes in v5:
time: 142 us; the launch traced here: 141 us
  Pallas kernels  136 us (96%)
  local copies, waits for them, and re-layouts  3.37 us (2%)
    pallas_call x1, Pallas kernels, local(): pl.pallas_call(functools.partial(kernel, sizes, blocks, columns * groups)...  136 us
  transfers between devices with their start and end apart: 1, of which 0 were waited for; matrix products, arithmetic and copies ran while one was open for 1% of the time, Pallas kernels for 0%

profile of v5, /device:TPU:8, one launch (start us, length us, event | category | flops | bytes accessed | tf_op | source)
XLA Modules:
  0.0 140.6 jit_solution(5064103450124836489)
XLA Ops:
  0.6 0.0 copy-start
  0.6 0.0 copy-start.3
  0.7 0.1 collective-permute-start
  0.8 0.6 copy-done.3
  1.3 0.1 copy.8
  1.4 0.1 reshape.98
  1.6 0.0 copy-done
  1.6 0.0 copy-start.1
  1.6 0.0 copy-start.2
  1.6 1.1 gather_fusion
  2.8 0.2 convert_reduce_fusion
  3.0 0.1 select_reduce_fusion
  3.2 0.0 collective-permute-done.their_start
  3.2 0.1 broadcast_in_dim.17.names
  3.2 0.0 copy-done.1
  3.3 0.0 copy-done.2
  3.3 136.1 %lanczos.1 = (f32[2,8,4096]{2,1,0:T(8,128)S(1)}, f32[4,16,16]{2,1,0:T(8,128)S(1)}) custom-call(bf16[64,64,128]{2,1,0:T(8,128)(2,1)S(1)} %copy-done.1, f32[8,4096]{1,0:T(8,128)S(1)} %copy-done.2, f32[8,4096]{1,0:T(8,128)S(1)} %collective-permute-done.their_start, f32[129,128]{1,0:T(8,128)S(1)} %broadcast_in_dim.17.names, ...), custom_call_target="tpu_custom_call" | custom-call | tf_op jit(solution)/shard_map/lanczos/pallas_call | solution.py:475
  139.3 0.7 copy.11
  140.0 0.6 copy.12
  (7 shorter events, 0.0 us)
Async XLA Ops:
  0.6 1.0 copy-start
  0.6 0.7 copy-start.3
  0.7 2.5 %collective-permute-start = (f32[8,4096]{1,0:T(8,128)}, f32[8,4096]{1,0:T(8,128)S(1)}, u32[]{:S(2)}, u32[]{:S(2)}) collective-permute-start(f32[8,4096]{1,0:T(8,128)} %start.1), channel_id=1, source_target_pairs={{0,1},{1,0},{2,3},{3,2},{4,5},{5,4},{6,7},{7,6},{8,9},{9,8},{10,11... | collective-permute-start | bytes 393224 | tf_op jit(solution)/shard_map/ppermute | solution.py:425
  1.6 1.6 %copy-start.1 = (bf16[64,64,128]{2,1,0:T(8,128)(2,1)S(1)}, bf16[64,64,128]{2,1,0:T(8,128)(2,1)}, u32[]{:S(2)}) copy-start(bf16[64,64,128]{2,1,0:T(8,128)(2,1)} %tiles.1) | copy-start | bytes 3145732
  1.6 1.6 %copy-start.2 = (f32[8,4096]{1,0:T(8,128)S(1)}, f32[8,4096]{1,0:T(8,128)}, u32[]{:S(2)}) copy-start(f32[8,4096]{1,0:T(8,128)} %start.1) | copy-start | bytes 393220

commit v6 on v5

--- a/solution.py
+++ b/solution.py
@@ -181,6 +181,10 @@
     return jnp.concatenate([x[:, :width], x[:, width : 2 * width]], axis=0)
 
 
+def beside(lines):
+    return jnp.concatenate([jnp.concatenate(line, axis=1) for line in lines], axis=0)
+
+
 def pieces(x):
     high = x.astype(BF16)
     rest = x - high.astype(F32)
@@ -209,7 +213,7 @@
     half = columns // 2
     own_half = pl.ds(pl.multiple_of(sub * half, 128), half)
     own_rows = pl.ds(pl.multiple_of(sub * 8, 8), 8)
-    totals = [Total(place, near.at[i], far.at[i], tsend.at[i], trecv.at[i]) for i in range(5)]
+    totals = [Total(place, near.at[i], far.at[i], tsend.at[i], trecv.at[i]) for i in range(4)]
 
     def pair(i, src, dst):
         return remote(src, dst, xsend.at[i], xrecv.at[i], place.other)
@@ -318,10 +322,11 @@
         lax.fori_loop(0, blocks, mirror, 0, unroll=4)
         parts[1].start(builder(1))
         parts[2].start(builder(2))
-        known = gram_of(stack[16:, own_half], stack[16:, own_half])
         if m:
-            known = jnp.concatenate([known[0:16], known[16:32, 16:32]], axis=1)
-        totals[3 + m].start(0, fold(known))
+            totals[1].start(1, totals[1].finish(0))
+        else:
+            known = gram_of(stack[16:, own_half], stack[16:, own_half])
+            totals[3].start(0, fold(known))
 
         parts[0].receive()
         parts[1].receive()
@@ -364,7 +369,25 @@
         swaps = [pair(2 + 2 * m + i, product.at[h], theirs.at[m, h]) for i, h in enumerate(halves)]
         for one in swaps:
             one.start()
-        totals[m + 3].start(1, totals[m + 3].finish(0))
+        row = lax.broadcasted_iota(jnp.int32, (16, 16), 0)
+        col = lax.broadcasted_iota(jnp.int32, (16, 16), 1)
+        eye = jnp.where(row == col, 1.0, 0.0).astype(F32)
+        if m:
+            qq = unfold(totals[3].finish(1), 16)
+            cross = unfold(totals[1].finish(1), 32)
+            rr, rq = cross[:, :16], cross[:, 16:]
+            first_gram = beside([[rr, rq], [rq.T, qq]])
+            alpha = qq - rq.T
+            keep = eye - alpha.T
+            mix = jnp.concatenate([-eye, keep], axis=1)
+            link, inverse = factor(dot_t(dot(mix, first_gram), mix))
+            kept = dot(inverse, keep)
+            full[...] = dot(jnp.concatenate([-inverse, kept], axis=1), first_stack[...])
+            coeffs[0] = alpha
+            coeffs[1] = link
+            bases[0] = full[own_rows, :] * math.sqrt(nodes)
+        else:
+            totals[3].start(1, totals[3].finish(0))
         for part in parts:
             part.sent()
 
@@ -386,34 +409,23 @@
         totals[m + 1].start(0, fold(gram_of(stack[0:16, own_half], stack[:, own_half])))
         swaps[1].wait()
         residual((1 - sub) * (blocks // 4))
-        totals[m + 1].start(1, totals[m + 1].finish(0))
-        known = unfold(totals[m + 3].finish(1), 48 if m else 16)
-        cross = unfold(totals[m + 1].finish(1), 48 if m else 32)
-        cut = [x[:, 16 * k : 16 * k + 16] for x in (cross, known) for k in range(x.shape[1] // 16)]
-        row = lax.broadcasted_iota(jnp.int32, (16, 16), 0)
-        col = lax.broadcasted_iota(jnp.int32, (16, 16), 1)
-        eye = jnp.where(row == col, 1.0, 0.0).astype(F32)
-        if m:
-            rr, rq, rp, qq, qp, pp = cut
-            lines = [[rr, rq, rp], [rq.T, qq, qp], [rp.T, qp.T, pp]]
-        else:
-            rr, rq, qq = cut
-            lines = [[rr, rq], [rq.T, qq]]
-        gram = jnp.concatenate([jnp.concatenate(line, axis=1) for line in lines], axis=0)
-        alpha = qq - rq.T
-        mix = [-eye, eye - alpha.T] + ([-coeffs[1]] if m else [])
-        mix = jnp.concatenate(mix, axis=1)
+        if not m:
+            second_stack[16:48] = first_stack[...]
+            continue
+        totals[2].start(1, totals[2].finish(0))
+        cross = unfold(totals[2].finish(1), 48)
+        tt, tr, tq = (cross[:, 16 * k : 16 * k + 16] for k in range(3))
+        gram = beside([[tt, tr, tq], [tr.T, rr, rq], [tq.T, rq.T, qq]])
+        zero = jnp.zeros((16, 16), F32)
+        lift = beside([[-inverse, kept, zero], [zero, -inverse, kept], [zero, zero, eye]])
+        gram = dot_t(dot(lift, gram), lift)
+        alpha = gram[16:32, 16:32] - gram[16:32, 0:16]
+        mix = jnp.concatenate([-eye, eye - alpha.T, -link], axis=1)
         upper, inverse = factor(dot_t(dot(mix, gram), mix))
-        coeffs[2 * m] = alpha
-        coeffs[2 * m + 1] = upper
-        following = dot(dot(inverse, mix), stack[...])
-        if m:
-            full[...] = following
-            bases[1] = full[own_rows, :] * math.sqrt(nodes)
-        else:
-            second_stack[16:32] = following
-            second_stack[32:48] = first_stack[16:32]
-            bases[0] = second_stack[pl.ds(pl.multiple_of(16 + sub * 8, 8), 8), :] * math.sqrt(nodes)
+        coeffs[2] = alpha
+        coeffs[3] = upper
+        full[...] = dot(dot(dot(inverse, mix), lift), stack[...])
+        bases[1] = full[own_rows, :] * math.sqrt(nodes)
 
 
 def local(sizes, upper_tiles, tile_clusters, cluster_slot, start_block):
@@ -459,10 +471,10 @@
         wide(groups * CAP * 8 + CAP * 8),
         wide(blocks * 8 + 8),
         wide(2, blocks * 8),
-        wide(5, nx * ny, 8),
-        wide(5, nz * 2, 8),
-        dma((5, 2)),
-        dma((5, 2)),
+        wide(4, nx * ny, 8),
+        wide(4, nz * 2, 8),
+        dma((4, 2)),
+        dma((4, 2)),
         dma,
         dma,
         dma,

time: 142 us -> 133 us (0.937)
  Pallas kernels: 136 us -> 126 us
    pallas_call x1, Pallas kernels: 136 us -> 126 us  [local(): pl.pallas_call(functools.partial(kernel, sizes, blocks, columns * groups)...]
where the time goes in v6:
time: 133 us; the launch traced here: 131 us
  Pallas kernels  126 us (95%)
  local copies, waits for them, and re-layouts  3.37 us (3%)
    pallas_call x1, Pallas kernels, local(): pl.pallas_call(functools.partial(kernel, sizes, blocks, columns * groups)...  126 us
  transfers between devices with their start and end apart: 1, of which 0 were waited for; matrix products, arithmetic and copies ran while one was open for 1% of the time, Pallas kernels for 0%

profile of v6, /device:TPU:8, one launch (start us, length us, event | category | flops | bytes accessed | tf_op | source)
XLA Modules:
  0.0 130.6 jit_solution(11325897837673093144)
XLA Ops:
  0.6 0.0 copy-start
  0.6 0.0 copy-start.3
  0.7 0.1 collective-permute-start
  0.8 0.6 copy-done.3
  1.3 0.1 copy.8
  1.4 0.1 reshape.98
  1.6 0.0 copy-done
  1.6 0.0 copy-start.1
  1.6 0.0 copy-start.2
  1.6 1.1 gather_fusion
  2.8 0.2 convert_reduce_fusion
  3.0 0.1 select_reduce_fusion
  3.2 0.0 collective-permute-done.their_start
  3.2 0.1 broadcast_in_dim.17.names
  3.2 0.0 copy-done.1
  3.3 0.0 copy-done.2
  3.3 126.0 %lanczos.1 = (f32[2,8,4096]{2,1,0:T(8,128)S(1)}, f32[4,16,16]{2,1,0:T(8,128)S(1)}) custom-call(bf16[64,64,128]{2,1,0:T(8,128)(2,1)S(1)} %copy-done.1, f32[8,4096]{1,0:T(8,128)S(1)} %copy-done.2, f32[8,4096]{1,0:T(8,128)S(1)} %collective-permute-done.their_start, f32[129,128]{1,0:T(8,128)S(1)} %broadcast_in_dim.17.names, ...), custom_call_target="tpu_custom_call" | custom-call | tf_op jit(solution)/shard_map/lanczos/pallas_call | solution.py:487
  129.3 0.7 copy.11
  130.0 0.6 copy.12
  (7 shorter events, 0.0 us)
Async XLA Ops:
  0.6 1.0 copy-start
  0.6 0.7 copy-start.3
  0.7 2.5 %collective-permute-start = (f32[8,4096]{1,0:T(8,128)}, f32[8,4096]{1,0:T(8,128)S(1)}, u32[]{:S(2)}, u32[]{:S(2)}) collective-permute-start(f32[8,4096]{1,0:T(8,128)} %start.1), channel_id=1, source_target_pairs={{0,1},{1,0},{2,3},{3,2},{4,5},{5,4},{6,7},{7,6},{8,9},{9,8},{10,11... | collective-permute-start | bytes 393224 | tf_op jit(solution)/shard_map/ppermute | solution.py:437
  1.6 1.6 %copy-start.1 = (bf16[64,64,128]{2,1,0:T(8,128)(2,1)S(1)}, bf16[64,64,128]{2,1,0:T(8,128)(2,1)}, u32[]{:S(2)}) copy-start(bf16[64,64,128]{2,1,0:T(8,128)(2,1)} %tiles.1) | copy-start | bytes 3145732
  1.6 1.6 %copy-start.2 = (f32[8,4096]{1,0:T(8,128)S(1)}, f32[8,4096]{1,0:T(8,128)}, u32[]{:S(2)}) copy-start(f32[8,4096]{1,0:T(8,128)} %start.1) | copy-start | bytes 393220

commit v7 on v6

--- a/solution.py
+++ b/solution.py
@@ -83,7 +83,8 @@
             signal(barrier, place.peer(i))
             return carry
 
-        lax.fori_loop(1, place.groups, greet, 0, unroll=8)
+        lax.fori_loop(place.groups // 2, place.groups, greet, 0, unroll=8)
+        lax.fori_loop(1, place.groups // 2, greet, 0, unroll=8)
         rest = [d for k, d in enumerate(place.line) if k % 2 == 0]
         count = place.groups - 1 + len(rest)
     else:
@@ -281,7 +282,8 @@
                 scaled[block_rows(2 * t + p), :] = pairs[p] * scale_of(2 * t + p)
             return carry
 
-        lax.fori_loop(0, blocks // 2, scale_blocks, 0, unroll=4)
+        if not m:
+            lax.fori_loop(0, blocks // 2, scale_blocks, 0, unroll=4)
 
         def mirror(b, carry):
             block = scaled[block_rows(b), :]
@@ -323,7 +325,8 @@
         parts[1].start(builder(1))
         parts[2].start(builder(2))
         if m:
-            totals[1].start(1, totals[1].finish(0))
+            totals[1].start(0, fold(gram_of(first_stack[0:16, own_half], first_stack[:, own_half])))
+            second_stack[16:48] = first_stack[...]
         else:
             known = gram_of(stack[16:, own_half], stack[16:, own_half])
             totals[3].start(0, fold(known))
@@ -348,6 +351,18 @@
             return carry
 
         lax.fori_loop(0, blocks, forward, 0, unroll=4)
+        def scatter(slots):
+            for j in range(8):
+                added = 0.0
+                for k in slots:
+                    rows = returned[pl.ds(8 * k + j, groups, stride=24), :].astype(BF16)
+                    added = added + jnp.dot(onehot[k], rows, preferred_element_type=F32)
+                lines = pl.ds(j, blocks, stride=8)
+                product[lines, :] = product[lines, :] + added
+
+        scatter((0,))
+        if m:
+            totals[1].start(1, totals[1].finish(0))
         parts[2].receive()
 
         def spread_last(d, carry):
@@ -356,37 +371,14 @@
             return carry
 
         lax.fori_loop(0, groups, spread_last, 0, unroll=4)
-        for j in range(8):
-            added = jnp.zeros((blocks, 128), F32)
-            for k in range(CAP):
-                rows = returned[pl.ds(8 * k + j, groups, stride=24), :].astype(BF16)
-                added = added + jnp.dot(onehot[k], rows, preferred_element_type=F32)
-            lines = pl.ds(j, blocks, stride=8)
-            product[lines, :] = product[lines, :] + added
+        scatter((1, 2))
 
         height = blocks * 4
         halves = [pl.ds(pl.multiple_of(s * height, 8), height) for s in (1 - sub, sub)]
         swaps = [pair(2 + 2 * m + i, product.at[h], theirs.at[m, h]) for i, h in enumerate(halves)]
         for one in swaps:
             one.start()
-        row = lax.broadcasted_iota(jnp.int32, (16, 16), 0)
-        col = lax.broadcasted_iota(jnp.int32, (16, 16), 1)
-        eye = jnp.where(row == col, 1.0, 0.0).astype(F32)
-        if m:
-            qq = unfold(totals[3].finish(1), 16)
-            cross = unfold(totals[1].finish(1), 32)
-            rr, rq = cross[:, :16], cross[:, 16:]
-            first_gram = beside([[rr, rq], [rq.T, qq]])
-            alpha = qq - rq.T
-            keep = eye - alpha.T
-            mix = jnp.concatenate([-eye, keep], axis=1)
-            link, inverse = factor(dot_t(dot(mix, first_gram), mix))
-            kept = dot(inverse, keep)
-            full[...] = dot(jnp.concatenate([-inverse, kept], axis=1), first_stack[...])
-            coeffs[0] = alpha
-            coeffs[1] = link
-            bases[0] = full[own_rows, :] * math.sqrt(nodes)
-        else:
+        if not m:
             totals[3].start(1, totals[3].finish(0))
         for part in parts:
             part.sent()
@@ -399,6 +391,8 @@
                 for p in range(2):
                     b = 2 * t + p
                     both.append((product[block_rows(b), :] + theirs[m, block_rows(b), :]) * scale_of(b))
+                    if not m:
+                        scaled[block_rows(b), :] = both[p] * scale_of(b)
                 stack[0:8, lanes], stack[8:16, lanes] = pair_up(both[0], both[1])
                 return carry
 
@@ -406,12 +400,28 @@
 
         swaps[0].wait()
         residual(sub * (blocks // 4))
-        totals[m + 1].start(0, fold(gram_of(stack[0:16, own_half], stack[:, own_half])))
+        if m:
+            totals[2].start(0, fold(gram_of(stack[0:16, own_half], stack[:, own_half])))
         swaps[1].wait()
         residual((1 - sub) * (blocks // 4))
         if not m:
-            second_stack[16:48] = first_stack[...]
             continue
+        row = lax.broadcasted_iota(jnp.int32, (16, 16), 0)
+        col = lax.broadcasted_iota(jnp.int32, (16, 16), 1)
+        eye = jnp.where(row == col, 1.0, 0.0).astype(F32)
+        qq = unfold(totals[3].finish(1), 16)
+        cross = unfold(totals[1].finish(1), 32)
+        rr, rq = cross[:, :16], cross[:, 16:]
+        first_gram = beside([[rr, rq], [rq.T, qq]])
+        alpha = qq - rq.T
+        keep = eye - alpha.T
+        mix = jnp.concatenate([-eye, keep], axis=1)
+        link, inverse = factor(dot_t(dot(mix, first_gram), mix))
+        kept = dot(inverse, keep)
+        full[...] = dot(jnp.concatenate([-inverse, kept], axis=1), first_stack[...])
+        coeffs[0] = alpha
+        coeffs[1] = link
+        bases[0] = full[own_rows, :] * math.sqrt(nodes)
         totals[2].start(1, totals[2].finish(0))
         cross = unfold(totals[2].finish(1), 48)
         tt, tr, tq = (cross[:, 16 * k : 16 * k + 16] for k in range(3))

time: 133 us -> 130 us (0.977)
  Pallas kernels: 126 us -> 123 us
    pallas_call x1, Pallas kernels: 126 us -> 123 us  [local(): pl.pallas_call(functools.partial(kernel, sizes, blocks, columns * groups)...]
where the time goes in v7:
time: 130 us; the launch traced here: 128 us
  Pallas kernels  123 us (95%)
  local copies, waits for them, and re-layouts  3.37 us (3%)
    pallas_call x1, Pallas kernels, local(): pl.pallas_call(functools.partial(kernel, sizes, blocks, columns * groups)...  123 us
  transfers between devices with their start and end apart: 1, of which 0 were waited for; matrix products, arithmetic and copies ran while one was open for 1% of the time, Pallas kernels for 0%

profile of v7, /device:TPU:8, one launch (start us, length us, event | category | flops | bytes accessed | tf_op | source)
XLA Modules:
  0.0 128.0 jit_solution(10715427651241708274)
XLA Ops:
  0.6 0.0 copy-start
  0.6 0.0 copy-start.3
  0.7 0.1 collective-permute-start
  0.8 0.6 copy-done.3
  1.3 0.1 copy.8
  1.4 0.1 reshape.98
  1.6 0.0 copy-done
  1.6 0.0 copy-start.1
  1.6 0.0 copy-start.2
  1.6 1.1 gather_fusion
  2.8 0.2 convert_reduce_fusion
  3.0 0.1 select_reduce_fusion
  3.2 0.0 collective-permute-done.their_start
  3.2 0.1 broadcast_in_dim.17.names
  3.2 0.0 copy-done.1
  3.3 0.0 copy-done.2
  3.3 123.4 %lanczos.1 = (f32[2,8,4096]{2,1,0:T(8,128)S(1)}, f32[4,16,16]{2,1,0:T(8,128)S(1)}) custom-call(bf16[64,64,128]{2,1,0:T(8,128)(2,1)S(1)} %copy-done.1, f32[8,4096]{1,0:T(8,128)S(1)} %copy-done.2, f32[8,4096]{1,0:T(8,128)S(1)} %collective-permute-done.their_start, f32[129,128]{1,0:T(8,128)S(1)} %broadcast_in_dim.17.names, ...), custom_call_target="tpu_custom_call" | custom-call | tf_op jit(solution)/shard_map/lanczos/pallas_call | solution.py:497
  126.7 0.7 copy.11
  127.4 0.6 copy.12
  (7 shorter events, 0.0 us)
Async XLA Ops:
  0.6 1.0 copy-start
  0.6 0.7 copy-start.3
  0.7 2.5 %collective-permute-start = (f32[8,4096]{1,0:T(8,128)}, f32[8,4096]{1,0:T(8,128)S(1)}, u32[]{:S(2)}, u32[]{:S(2)}) collective-permute-start(f32[8,4096]{1,0:T(8,128)} %start.1), channel_id=1, source_target_pairs={{0,1},{1,0},{2,3},{3,2},{4,5},{5,4},{6,7},{7,6},{8,9},{9,8},{10,11... | collective-permute-start | bytes 393224 | tf_op jit(solution)/shard_map/ppermute | solution.py:447
  1.6 1.6 %copy-start.1 = (bf16[64,64,128]{2,1,0:T(8,128)(2,1)S(1)}, bf16[64,64,128]{2,1,0:T(8,128)(2,1)}, u32[]{:S(2)}) copy-start(bf16[64,64,128]{2,1,0:T(8,128)(2,1)} %tiles.1) | copy-start | bytes 3145732
  1.6 1.6 %copy-start.2 = (f32[8,4096]{1,0:T(8,128)S(1)}, f32[8,4096]{1,0:T(8,128)}, u32[]{:S(2)}) copy-start(f32[8,4096]{1,0:T(8,128)} %start.1) | copy-start | bytes 393220

commit v8 on v7

--- a/solution.py
+++ b/solution.py
@@ -262,11 +262,11 @@
     degree[...] = own_degree[...] + jnp.where(is_low(sums_in.shape), sums_in, swap(sums_in))
     swap_degree = pair(1, degree, their_degree)
     swap_degree.start()
-    sent_columns.sent()
+    _, inverse = factor(unfold(totals[0].finish(1), 16))
+    first_stack[16:32] = dot(inverse, full[...])
     swap_degree.wait()
     scale[...] = lax.rsqrt(degree[...] + their_degree[...])
-    _, inverse = factor(unfold(totals[0].finish(1), 16))
-    first_stack[16:32] = dot(inverse, full[...])
+    sent_columns.sent()
 
     def scale_of(b):
         return jnp.broadcast_to(scale[pl.ds(b, 1), :], (8, 128))

time: 130 us -> 129 us (level)
    pallas_call x1, Pallas kernels: 123 us -> 122 us  [local(): pl.pallas_call(functools.partial(kernel, sizes, blocks, columns * groups)...]
where the time goes in v8:
time: 129 us; the launch traced here: 126 us
  Pallas kernels  122 us (95%)
  local copies, waits for them, and re-layouts  3.37 us (3%)
    pallas_call x1, Pallas kernels, local(): pl.pallas_call(functools.partial(kernel, sizes, blocks, columns * groups)...  122 us
  transfers between devices with their start and end apart: 1, of which 0 were waited for; matrix products, arithmetic and copies ran while one was open for 1% of the time, Pallas kernels for 0%

profile of v8, /device:TPU:8, one launch (start us, length us, event | category | flops | bytes accessed | tf_op | source)
XLA Modules:
  0.0 126.5 jit_solution(2385675464398604569)
XLA Ops:
  0.6 0.0 copy-start
  0.6 0.0 copy-start.3
  0.7 0.1 collective-permute-start
  0.8 0.6 copy-done.3
  1.3 0.1 copy.8
  1.4 0.1 reshape.98
  1.6 0.0 copy-done
  1.6 0.0 copy-start.1
  1.6 0.0 copy-start.2
  1.6 1.1 gather_fusion
  2.8 0.2 convert_reduce_fusion
  3.0 0.1 select_reduce_fusion
  3.2 0.0 collective-permute-done.their_start
  3.2 0.1 broadcast_in_dim.17.names
  3.2 0.0 copy-done.1
  3.3 0.0 copy-done.2
  3.3 121.9 %lanczos.1 = (f32[2,8,4096]{2,1,0:T(8,128)S(1)}, f32[4,16,16]{2,1,0:T(8,128)S(1)}) custom-call(bf16[64,64,128]{2,1,0:T(8,128)(2,1)S(1)} %copy-done.1, f32[8,4096]{1,0:T(8,128)S(1)} %copy-done.2, f32[8,4096]{1,0:T(8,128)S(1)} %collective-permute-done.their_start, f32[129,128]{1,0:T(8,128)S(1)} %broadcast_in_dim.17.names, ...), custom_call_target="tpu_custom_call" | custom-call | tf_op jit(solution)/shard_map/lanczos/pallas_call | solution.py:497
  125.2 0.7 copy.11
  125.9 0.6 copy.12
  (7 shorter events, 0.0 us)
Async XLA Ops:
  0.6 1.0 copy-start
  0.6 0.7 copy-start.3
  0.7 2.5 %collective-permute-start = (f32[8,4096]{1,0:T(8,128)}, f32[8,4096]{1,0:T(8,128)S(1)}, u32[]{:S(2)}, u32[]{:S(2)}) collective-permute-start(f32[8,4096]{1,0:T(8,128)} %start.1), channel_id=1, source_target_pairs={{0,1},{1,0},{2,3},{3,2},{4,5},{5,4},{6,7},{7,6},{8,9},{9,8},{10,11... | collective-permute-start | bytes 393224 | tf_op jit(solution)/shard_map/ppermute | solution.py:447
  1.6 1.6 %copy-start.1 = (bf16[64,64,128]{2,1,0:T(8,128)(2,1)S(1)}, bf16[64,64,128]{2,1,0:T(8,128)(2,1)}, u32[]{:S(2)}) copy-start(bf16[64,64,128]{2,1,0:T(8,128)(2,1)} %tiles.1) | copy-start | bytes 3145732
  1.6 1.6 %copy-start.2 = (f32[8,4096]{1,0:T(8,128)S(1)}, f32[8,4096]{1,0:T(8,128)}, u32[]{:S(2)}) copy-start(f32[8,4096]{1,0:T(8,128)} %start.1) | copy-start | bytes 393220
